TPU v7x, 32 devices: a whole 2x2x4 slice. The times are simulated.
32 devices in a mesh: seq: 2 (over core), ctx: 4 (over z), fsdp: 4 (over y, x).
Axes of the slice: x: 2, y: 2, z: 4, core: 2. Of those that a mesh axis runs over, the one named last changes fastest.
Arguments:
- tokens: bfloat16 [8, 512, 2048], P(('seq', 'fsdp'), 'ctx'), may hold values from -6 to 6
- stretch_order: int32 [8], replicated, may hold values from 0 to 7, as said below
- expert_ids: int32 [8, 512, 8], P(('seq', 'fsdp'), 'ctx'), may hold values from 0 to 31, as said below
- slot_index: int32 [8, 512, 8], P(('seq', 'fsdp'), 'ctx'), may hold values from 0 to 33, as said below
- norm_attn: bfloat16 [2048], P(('seq', 'ctx', 'fsdp')), may hold values from 0.5 to 1.5
- head_gains: bfloat16 [2, 128], replicated, may hold values from 0.5 to 1.5
- w_query: bfloat16 [2048, 4096], P(('seq', 'ctx', 'fsdp')), may hold values from -0.125 to 0.125
- key_projection_weight: bfloat16 [2048, 512], P(('seq', 'ctx', 'fsdp')), may hold values from -0.125 to 0.125
- value_projection_weight: bfloat16 [2048, 512], P(('seq', 'ctx', 'fsdp')), may hold values from -0.125 to 0.125
- w_out: bfloat16 [4096, 2048], P(('seq', 'ctx', 'fsdp')), may hold values from -0.375 to 0.375
- norm_moe: bfloat16 [2048], P(('seq', 'ctx', 'fsdp')), may hold values from 0.5 to 1.5
- w_router: bfloat16 [2048, 32], P(('seq', 'ctx', 'fsdp')), may hold values from -0.06591797 to 0.06591797
- w_gate: bfloat16 [32, 2048, 768], P(('seq', 'ctx', 'fsdp')), may hold values from -0.125 to 0.125
- w_up: bfloat16 [32, 2048, 768], P(('seq', 'ctx', 'fsdp')), may hold values from -0.125 to 0.125
- w_down: bfloat16 [32, 768, 2048], P(('seq', 'ctx', 'fsdp')), may hold values from -0.625 to 0.625
- cotangent: bfloat16 [8, 512, 2048], P(('seq', 'fsdp'), 'ctx'), may hold values from -6 to 6
Outputs:
- layer_out: bfloat16 [8, 512, 2048], P(('seq', 'fsdp'), 'ctx')
- grad_tokens: bfloat16 [8, 512, 2048], P(('seq', 'fsdp'), 'ctx')
- grad_norm_attn: float32 [2048], P(('seq', 'ctx', 'fsdp'))
- grad_head_gains: float32 [2, 128], replicated
- grad_w_query: float32 [2048, 4096], P(('seq', 'ctx', 'fsdp'))
- grad_w_key: float32 [2048, 512], P(('seq', 'ctx', 'fsdp'))
- grad_w_value: float32 [2048, 512], P(('seq', 'ctx', 'fsdp'))
- grad_w_out: float32 [4096, 2048], P(('seq', 'ctx', 'fsdp'))
- grad_norm_moe: float32 [2048], P(('seq', 'ctx', 'fsdp'))
- grad_w_router: float32 [2048, 32], P(('seq', 'ctx', 'fsdp'))
- grad_w_gate: float32 [32, 2048, 768], P(('seq', 'ctx', 'fsdp'))
- grad_w_up: float32 [32, 2048, 768], P(('seq', 'ctx', 'fsdp'))
- grad_w_down: float32 [32, 768, 2048], P(('seq', 'ctx', 'fsdp'))
Inputs may be any that keep to these rules, and one draw needn't show every extreme that they name: `stretch_order`: A permutation; stored block 2 i and block 2 i + 1 of 64 rows hold block numbers that add to 7. `expert_ids`: each token names 8 different experts; expert e is held by index e of the seq+ctx+fsdp axes. `slot_index`: over the 128 rows of one device, tokens in order, a choice's slot is the number of earlier choices of that device naming the same expert, or 33 where that number is 33 or more (the choice is dropped); some expert has more than 33 choices from every device.
All inputs are finite; a program needn't handle non-finite values.
Results may differ from a plain program's by a relative error of at most 0.025.
Values may be sent and summed in bfloat16 or wider, within the bound.
A program may use at most 256 MiB of HBM per device.

v0:
```python
import functools

import jax
import jax.numpy as jnp
import numpy as np
from jax import lax
from jax.experimental import pallas as pl
from jax.experimental.pallas import tpu as pltpu
from jax.sharding import PartitionSpec as P

QUERY_HEADS = 32
KEY_VALUE_HEADS = 4
HEAD_DIM = 128
TOP = 8
AXES = ("seq", "ctx", "fsdp")
MESH = pl.DeviceIdType.MESH
epsilon = 1e-06
rope_base = 1000000.0
VMEM_LIMIT = 56 * 2**20
f32 = jnp.float32
bf16 = jnp.bfloat16


def round_up(value, step):
    return (value + step - 1) // step * step


def place():
    return tuple(lax.axis_index(name) for name in AXES)


def sizes():
    return tuple(lax.axis_size(name) for name in AXES)


def signal(device):
    pl.semaphore_signal(
        pltpu.get_barrier_semaphore(), inc=1, device_id=device, device_id_type=MESH
    )


def remote(src, dst, send, recv, device):
    return pltpu.make_async_remote_copy(
        src_ref=src,
        dst_ref=dst,
        send_sem=send,
        recv_sem=recv,
        device_id=device,
        device_id_type=MESH,
    )


def params(cid, limit=VMEM_LIMIT):
    return pltpu.CompilerParams(
        collective_id=cid, has_side_effects=True, vmem_limit_bytes=limit
    )


ANY = pl.BlockSpec(memory_space=pl.ANY)
DMA = pltpu.SemaphoreType.DMA


def rms_unit(rows):
    factor = lax.rsqrt(jnp.mean(rows * rows, axis=-1, keepdims=True) + epsilon)
    return rows * factor, factor


def norm_backward(grad_scaled, normed, factor, gain):
    grad_normed = grad_scaled * gain
    inner = jnp.mean(grad_normed * normed, axis=-1, keepdims=True)
    return factor * (grad_normed - normed * inner)


def half_turn(rows, cosine, sine):
    return rows * cosine + pltpu.roll(rows, HEAD_DIM // 2, 1) * sine


def score_block(qr, kr, pos_col, pos_row):
    scores = lax.dot_general(
        qr, kr, (((1,), (1,)), ((), ())), preferred_element_type=f32
    ) * (HEAD_DIM**-0.5)
    scores = jnp.where(pos_col >= pos_row, scores, -jnp.inf)
    peak = jnp.max(scores, axis=-1, keepdims=True)
    weight = jnp.exp(scores - peak)
    return weight * (1.0 / jnp.sum(weight, axis=-1, keepdims=True))


def z_neighbours():
    _, C, _ = sizes()
    s, c, f = place()
    return [(s, lax.rem(c + k, C), f) for k in range(1, C)]


def plane_neighbours():
    S, _, F = sizes()
    s, c, f = place()
    Q = S * F
    at = [lax.rem(s * F + f + k, Q) for k in range(1, Q)]
    return at, [(q // F, c, lax.rem(q, F)) for q in at]


def greet_all(peers):
    for peer in peers:
        signal(peer)
    pl.semaphore_wait(pltpu.get_barrier_semaphore(), len(peers))


class Line:
    def __init__(self, own, block, rsend, rrecv, lsend, lrecv):
        s, self.c, f = place()
        self.C = lax.axis_size("ctx")
        self.own, self.block = own, block
        self.sems = (rsend, rrecv, lsend, lrecv)
        self.right = (s, lax.rem(self.c + 1, self.C), f)
        self.left = (s, lax.rem(self.c + self.C - 1, self.C), f)

    def copy(self, rightward, h):
        origin = self.c - h if rightward else self.c + h
        src = self.own if h == 0 else self.block(origin)
        send, recv = self.sems[:2] if rightward else self.sems[2:]
        return remote(
            src, self.block(origin), send.at[h], recv.at[h], self.right if rightward else self.left
        )

    def sends(self, rightward, h):
        if rightward:
            return jnp.logical_and(self.c >= h, self.c < self.C - 1)
        return jnp.logical_and(self.c + h < self.C, self.c > 0)

    def start(self):
        for way in (True, False):
            pl.when(self.sends(way, 0))(self.copy(way, 0).start)

    def hop(self, h):
        for way in (True, False):
            origin = self.c - h if way else self.c + h
            there = origin >= 0 if way else origin < self.C
            landed = remote(
                self.block(origin), self.block(origin),
                self.sems[0 if way else 2].at[h - 1], self.sems[1 if way else 3].at[h - 1],
                self.left if way else self.right,
            )
            pl.when(there)(landed.wait_recv)
            if h < self.C - 1:
                pl.when(self.sends(way, h))(self.copy(way, h).start)

    def finish(self):
        for way in (True, False):
            for h in range(self.C - 1):
                pl.when(self.sends(way, h))(self.copy(way, h).wait_send)


def line_sems(C):
    return [DMA((C - 1,)) for _ in range(4)]


def front_kernel(
    block, capacity, packed, experts,
    order, ids, slot_ids, tokens, wq, wk, wv, wo, router, norm_attn, norm_moe, cot, low_gains, frequency,
    X_out, W_out, WO_out, PK, SM, G, out_out, q_out, k_out, v, mixed_out, xnt_out, gain_attn, gain_moe, gains,
    cosine, sine, pos_col, pos_row, select_out, select_t_out, chosen, kept,
    X, W, WO, xn, kr, pack, out, q, mixed, xnt, select, select_t,
    local, save, zsend, zrecv, fsend, frecv, csend, crecv, wsend, wrecv,
    xrs, xrr, xls, xlr, grs, grr, gls, glr,
):
    S, C, F = sizes()
    s, c, f = place()
    Q = S * F
    rows, width = tokens.shape
    length = C * rows
    head_width = wq.shape[1] // C
    shard = wq.shape[0]
    wide = chosen.shape[1]
    z_peers = z_neighbours()
    f_peers = [(s, c, lax.rem(f + k, F)) for k in range(1, F)]
    sibling = (1 - s, c, f)
    pair = s * C + c
    out_dst = (lax.rem(pair, S), pair // S, f)
    pair_in = c * S + s
    out_src = (pair_in // C, lax.rem(pair_in, C), f)
    stays = jnp.logical_and(out_dst[0] == s, out_dst[1] == c)
    moves = jnp.logical_not(stays)
    greet = (
        jnp.where(stays, 1 - s, out_src[0]),
        jnp.where(stays, C - 1 - c, out_src[1]),
        f,
    )
    def as_column(line):
        size = line.shape[1]
        square = lax.broadcasted_iota(jnp.int32, (size, size), 0) == lax.broadcasted_iota(
            jnp.int32, (size, size), 1
        )
        return jnp.sum(jnp.where(square, line, 0.0), axis=1, keepdims=True)

    lane = lax.broadcasted_iota(jnp.int32, (rows, wide), 1).astype(f32)
    hits = jnp.zeros((rows, wide), f32)
    slot_map = jnp.full((rows, wide), -1.0, f32)
    for j in range(TOP):
        here = lane == as_column(ids[j : j + 1, :].astype(f32))
        slot = jnp.broadcast_to(as_column(slot_ids[j : j + 1, :].astype(f32)), (rows, wide))
        hits = jnp.where(here, 1.0, hits)
        slot_map = jnp.where(jnp.logical_and(here, slot < capacity), slot, slot_map)
    lane = lax.broadcasted_iota(jnp.int32, pack.shape, 1)
    own_lane = lax.broadcasted_iota(jnp.int32, (experts, pack.shape[1]), 0) == lax.broadcasted_iota(
        jnp.int32, (experts, pack.shape[1]), 1
    )
    packed_rows = lax.dot_general(
        router[...], own_lane.astype(bf16), (((0,), (0,)), ((), ())), preferred_element_type=f32
    )
    for i, line in enumerate((norm_attn, norm_moe)):
        packed_rows = jnp.where(lane == experts + i, as_column(line[...].astype(f32)), packed_rows)
    pack[...] = packed_rows.astype(bf16)
    gains[...] = low_gains[...].astype(f32)
    chosen[...] = hits
    kept[...] = (slot_map >= 0.0).astype(f32)
    SM[c] = slot_map
    greet_all(z_peers + f_peers + [sibling, greet])

    def pieces(target):
        kv = (target * KEY_VALUE_HEADS) // C
        q_cols = pl.ds(pl.multiple_of(target * head_width, 128), head_width)
        kv_cols = pl.ds(pl.multiple_of(kv * HEAD_DIM, 128), HEAD_DIM)
        mine = W.at[s, c, f]
        return [
            (wq.at[:, q_cols], mine.at[:, pl.ds(0, head_width)]),
            (wk.at[:, kv_cols], mine.at[:, pl.ds(head_width, HEAD_DIM)]),
            (wv.at[:, kv_cols], mine.at[:, pl.ds(head_width + HEAD_DIM, HEAD_DIM)]),
            (pack, PK.at[s, c, f]),
        ]

    def token_rows(at):
        return X.at[pl.ds(pl.multiple_of(at * rows, 16), rows)]

    own = [
        pltpu.make_async_copy(src, dst, local.at[i])
        for i, (src, dst) in enumerate(pieces(c) + [(tokens, token_rows(c)), (cot, G.at[c])])
    ]
    z_copies = [
        remote(src, dst, zsend.at[i, k], zrecv.at[i, k], peer)
        for k, peer in enumerate(z_peers)
        for i, (src, dst) in enumerate(pieces(peer[1]))
    ]
    slot_copies = [
        remote(SM.at[c], SM.at[c], zsend.at[4, k], zrecv.at[4, k], peer)
        for k, peer in enumerate(z_peers)
    ]
    x_line = Line(tokens, token_rows, xrs, xrr, xls, xlr)
    g_line = Line(cot, lambda at: G.at[at], grs, grr, gls, glr)
    out_copy = remote(wo, WO.at[out_dst[0], f], wsend.at[0], wrecv.at[0], out_dst)
    out_stay = pltpu.make_async_copy(wo, WO.at[s, f], wsend.at[1])
    for copy in own + z_copies + slot_copies:
        copy.start()
    x_line.start()
    pl.when(moves)(out_copy.start)
    pl.when(stays)(out_stay.start)

    where = lax.broadcasted_iota(jnp.int32, (1, length), 1)
    where_col = lax.broadcasted_iota(jnp.int32, (length, 1), 0)
    stretch_rows = rows // 2

    def position(at):
        total = jnp.zeros_like(at)
        for j in range(2 * C):
            base = order[j] * stretch_rows - j * stretch_rows
            total = jnp.where(at // stretch_rows == j, at + base, total)
        return total

    pos_row[...] = position(where)
    pos_col[...] = position(where_col)
    angles = pos_col[...].astype(f32) * frequency[...]
    cosine[...] = jnp.cos(angles)
    turned = jnp.sin(angles)
    sine[...] = jnp.where(
        lax.broadcasted_iota(jnp.int32, turned.shape, 1) < HEAD_DIM // 2, -turned, turned
    )

    for copy in own[:5] + z_copies:
        copy.wait()

    def weight_block(index, at):
        return (W.at[s, :, at], PK.at[s, :, at], WO.at[s, at])[index]

    f_copies = [
        [
            remote(weight_block(i, f), weight_block(i, f), fsend.at[i, k], frecv.at[i, k], peer)
            for k, peer in enumerate(f_peers)
        ]
        for i in range(3)
    ]

    def to_sibling(i, k):
        at = lax.rem(f + F - k, F)
        return remote(weight_block(i, at), weight_block(i, at), csend.at[i, k], crecv.at[i, k], sibling)

    c_copies = [[to_sibling(i, k) for k in range(F)] for i in range(3)]
    for i in range(2):
        for copy in f_copies[i] + c_copies[i][:1]:
            copy.start()
    x_line.hop(1)
    for h in range(2, C - 1):
        x_line.hop(h)
    pl.when(moves)(out_copy.wait)
    pl.when(stays)(out_stay.wait)
    for copy in f_copies[2] + c_copies[2][:1]:
        copy.start()
    for k in range(F - 1):
        for i in range(2):
            f_copies[i][k].wait_recv()
            c_copies[i][k + 1].start()
    for copy in slot_copies:
        copy.wait()
    at = lax.broadcasted_iota(jnp.int32, (wide, Q * packed), 1) // packed
    expert = (at // F * C + c) * F + lax.rem(at, F)
    spread = (lax.broadcasted_iota(jnp.int32, (wide, Q * packed), 0) == expert).astype(bf16)
    slot_rows = SM[...].reshape(length, wide).astype(bf16)
    by_token = jnp.dot(slot_rows, spread, preferred_element_type=f32)
    base = (lax.broadcasted_iota(jnp.int32, by_token.shape, 0) // rows * capacity).astype(f32)
    number = lax.rem(lax.broadcasted_iota(jnp.int32, by_token.shape, 1), packed).astype(f32)
    select_t[...] = jnp.where(
        jnp.logical_and(by_token >= 0.0, by_token + base == number), 1.0, 0.0
    ).astype(bf16)
    at = lax.broadcasted_iota(jnp.int32, (Q, wide), 0)
    expert = (at // F * C + c) * F + lax.rem(at, F)
    spread = (lax.broadcasted_iota(jnp.int32, (Q, wide), 1) == expert).astype(bf16)
    by_slot = lax.dot_general(
        spread, slot_rows, (((1,), (1,)), ((), ())), preferred_element_type=f32
    )
    base = (where // rows * capacity).astype(f32)
    by_slot = jnp.where(by_slot >= 0.0, by_slot + base, -1.0)
    number = lax.broadcasted_iota(jnp.int32, (packed, length), 0).astype(f32)
    for p in range(Q):
        select[p * packed : (p + 1) * packed, :] = jnp.where(
            number == by_slot[p : p + 1, :], 1.0, 0.0
        ).astype(bf16)

    x_line.hop(C - 1)
    g_line.start()
    for i in range(2):
        for copy in c_copies[i]:
            copy.wait()
    saves = [
        pltpu.make_async_copy(src, dst, save.at[i])
        for i, (src, dst) in enumerate(
            (
                (X, X_out), (W, W_out), (select, select_out), (select_t, select_t_out),
                (WO, WO_out), (q, q_out), (mixed, mixed_out), (out, out_out), (xnt, xnt_out),
            )
        )
    ]
    for copy in saves[:4]:
        copy.start()
    across = lax.broadcasted_iota(jnp.int32, (HEAD_DIM, HEAD_DIM), 0)
    diagonal = across == lax.broadcasted_iota(jnp.int32, (HEAD_DIM, HEAD_DIM), 1)
    flat = PK[...].reshape(width, PK.shape[-1]).astype(f32)
    for j in range(width // HEAD_DIM):
        part = slice(j * HEAD_DIM, (j + 1) * HEAD_DIM)
        for i, row in enumerate((gain_attn, gain_moe)):
            line = flat[part, experts + i : experts + i + 1]
            row[:, part] = jnp.sum(jnp.where(diagonal, line, 0.0), axis=0, keepdims=True)

    def norm_rows(i, carry):
        part = pl.ds(i * 64, 64)
        unit, _ = rms_unit(X[part, :].astype(f32))
        xn[part, :] = (unit * gain_attn[...]).astype(bf16)
        return carry

    lax.fori_loop(0, length // 64, norm_rows, 0)

    def weights(cols):
        return W[:, :, :, :, cols].reshape(width, 2 * HEAD_DIM)

    kv = jnp.dot(xn[...], weights(pl.ds(head_width, 2 * HEAD_DIM)), preferred_element_type=f32)
    k_out[...] = kv[:, :HEAD_DIM]
    v[...] = kv[:, HEAD_DIM:].astype(bf16)
    unit, _ = rms_unit(k_out[...])
    kr[...] = half_turn(unit * gains[1:2, :], cosine[...], sine[...]).astype(bf16)

    def head_pair(i, carry):
        cols = pl.ds(pl.multiple_of(i * 2 * HEAD_DIM, 2 * HEAD_DIM), 2 * HEAD_DIM)
        both = jnp.dot(xn[...], weights(cols), preferred_element_type=f32)
        q[:, cols] = both
        for half in range(2):
            lanes = pl.ds(pl.multiple_of((2 * i + half) * HEAD_DIM, HEAD_DIM), HEAD_DIM)
            for part in range(length // block):
                at = slice(part * block, (part + 1) * block)
                unit, _ = rms_unit(both[at, half * HEAD_DIM : (half + 1) * HEAD_DIM])
                qr = half_turn(unit * gains[0:1, :], cosine[at, :], sine[at, :]).astype(bf16)
                probs = score_block(qr, kr[...], pos_col[at, :], pos_row[...])
                mixed[at, lanes] = jnp.dot(
                    probs.astype(bf16), v[...], preferred_element_type=f32
                ).astype(bf16)
        return carry

    pairs = head_width // (2 * HEAD_DIM)
    half_way = pairs // 2
    hops = {}
    for h in range(1, C - 1):
        hops.setdefault(min(pairs, 1 + (h - 1) * pairs // (C - 2)), []).append(h)
    done = 0
    for stop in sorted(set(hops) | {half_way, pairs}):
        lax.fori_loop(done, stop, head_pair, 0)
        done = stop
        for h in hops.get(stop, ()):
            g_line.hop(h)
        if stop == half_way:
            for k in range(F - 1):
                f_copies[2][k].wait_recv()
                c_copies[2][k + 1].start()
    for copy in c_copies[2]:
        copy.wait()
    for copy in saves[4:7]:
        copy.start()

    def project(j, carry):
        cols = pl.ds(pl.multiple_of(j * 256, 256), 256)
        out[:, cols] = jnp.dot(
            mixed[...], WO[:, :, :, cols].reshape(head_width, 256), preferred_element_type=f32
        ).astype(bf16)
        return carry

    lax.fori_loop(0, width // 256, project, 0)
    saves[7].start()

    def turn(j, carry):
        cols = pl.ds(pl.multiple_of(j * 256, 256), 256)
        xnt[cols, :] = xn[:, cols].T
        return carry

    lax.fori_loop(0, width // 256, turn, 0)
    saves[8].start()
    g_line.hop(C - 1)
    x_line.finish()
    g_line.finish()
    for line in f_copies:
        for copy in line:
            copy.wait_send()
    for copy in saves + own[5:]:
        copy.wait()


def front(
    capacity, packed, order, ids, slot_ids, tokens, wq, wk, wv, wo, router, norm_attn, norm_moe, cot, gains
):
    S, C, F = sizes()
    Q = S * F
    rows, width = tokens.shape
    length = C * rows
    shard = wq.shape[0]
    head_width = wq.shape[1] // C
    experts = router.shape[0]
    wide = round_up(experts, 128)
    frequency = np.power(rope_base, -np.arange(HEAD_DIM // 2) * 2.0 / HEAD_DIM)
    frequency = jnp.asarray(np.tile(frequency, 2)[None].astype(np.float32))
    block = min(length, 512)
    sds = jax.ShapeDtypeStruct
    V = pltpu.VMEM
    vm = pl.BlockSpec(memory_space=pltpu.VMEM)
    w_shape = (S, C, F, shard, head_width + 2 * HEAD_DIM)
    wo_shape = (S, F) + wo.shape
    pack_block = (shard, round_up(experts + 2, 128))
    pack_shape = (S, C, F) + pack_block
    return pl.pallas_call(
        functools.partial(front_kernel, block, capacity, packed, experts),
        out_shape=[
            sds((length, width), bf16),
            sds(w_shape, bf16),
            sds(wo_shape, bf16),
            sds(pack_shape, bf16),
            sds((C, rows, wide), f32),
            sds((C, rows, width), bf16),
            sds((length, width), bf16),
            sds((length, head_width), f32),
            sds((length, HEAD_DIM), f32),
            sds((length, HEAD_DIM), bf16),
            sds((length, head_width), bf16),
            sds((width, length), bf16),
            sds((1, width), f32),
            sds((1, width), f32),
            sds(gains.shape, f32),
            sds((length, HEAD_DIM), f32),
            sds((length, HEAD_DIM), f32),
            sds((length, 1), jnp.int32),
            sds((1, length), jnp.int32),
            sds((Q * packed, length), bf16),
            sds((length, Q * packed), bf16),
            sds((rows, wide), f32),
            sds((rows, wide), f32),
        ],
        in_specs=[pl.BlockSpec(memory_space=pltpu.SMEM), vm, vm] + [ANY] * 5 + [vm] * 3 + [ANY, vm, vm],
        out_specs=[ANY] * 3 + [vm, vm] + [ANY] * 3 + [vm] * 2 + [ANY] * 2 + [vm] * 7 + [ANY] * 2 + [vm] * 2,
        scratch_shapes=[
            V((length, width), bf16),
            V(w_shape, bf16),
            V(wo_shape, bf16),
            V((length, width), bf16),
            V((length, HEAD_DIM), bf16),
            V(pack_block, bf16),
            V((length, width), bf16),
            V((length, head_width), f32),
            V((length, head_width), bf16),
            V((width, length), bf16),
            V((Q * packed, length), bf16),
            V((length, Q * packed), bf16),
            DMA((6,)), DMA((9,)),
            DMA((5, C - 1)), DMA((5, C - 1)),
            DMA((3, F - 1)), DMA((3, F - 1)),
            DMA((3, F)), DMA((3, F)),
            DMA((2,)), DMA((1,)),
        ]
        + line_sems(C)
        + line_sems(C),
        name="gather_and_attend",
        compiler_params=params(1, 60 * 2**20),
    )(order, ids, slot_ids, tokens, wq, wk, wv, wo, router, norm_attn, norm_moe, cot, gains, frequency)


CHUNKS = 8


def columns(width, j):
    step = width // CHUNKS
    return pl.ds(j * step, step)


def three_parts(line):
    high = line.astype(bf16).astype(f32)
    rest = line - high
    middle = rest.astype(bf16).astype(f32)
    row = lax.broadcasted_iota(jnp.int32, (16, line.shape[1]), 0)
    rows = jnp.where(row == 0, high, jnp.where(row == 1, middle, jnp.where(row == 2, rest - middle, 0.0)))
    return rows.astype(bf16)


def halves(total):
    return total // 2


def dispatch_kernel(
    packed, out_part, G_in, tokens, pack, gain, chosen, kept, select, w_gate, w_up, w_down,
    buffer_out, gbuf, wrow, h1, xm, gates, hidden_out, dgp_out, dup_out, dgr,
    OP, RB, XM, SL, WM, WS, G, SG, buffer, WG, WU, WD, gp, up, gw, dup,
    local, load, saved, osend, orecv, gsend, grecv, xsend, xrecv, msend, mrecv, bsend, brecv, wsend, wrecv,
):
    S, C, F = sizes()
    s, c, f = place()
    Q = S * F
    q = s * F + f
    rows, width = tokens.shape
    total_rows = Q * packed
    half = halves(total_rows)
    z_peers = z_neighbours()
    p_at, p_peers = plane_neighbours()
    loads = [
        pltpu.make_async_copy(G_in, G, load.at[0]),
        pltpu.make_async_copy(w_down.at[0], WD, load.at[1]),
        pltpu.make_async_copy(w_gate.at[0], WG, load.at[2]),
        pltpu.make_async_copy(w_up.at[0], WU, load.at[3]),
    ]
    for copy in loads:
        copy.start()
    greet_all(z_peers + p_peers)
    mine = pl.ds(pl.multiple_of(q * packed, 16), packed)
    own_rows = pl.ds(pl.multiple_of(c * rows, 16), rows)
    right = (s, lax.rem(c + 1, C), f)
    left = (s, lax.rem(c + C - 1, C), f)

    def rightward(t):
        return remote(OP.at[t], RB.at[t], osend.at[0, t], orecv.at[0, t], right)

    def leftward(t):
        return remote(OP.at[t], RB.at[jnp.where(c - 1 == t, C, t)], osend.at[1, t], orecv.at[1, t], left)

    def merge(t, way):
        remote(OP.at[t], RB.at[t], osend.at[way, t], orecv.at[way, t], left).wait_recv()

        def add(j, carry):
            part = pl.ds(j * 32, 32)
            OP[t, part, :] = (OP[t, part, :].astype(f32) + RB[t, part, :].astype(f32)).astype(bf16)
            return carry

        lax.fori_loop(0, rows // 32, add, 0)

    def pass_on(step):
        t_right = C - 1 + c - step
        t_left = step - (C - 1 - c)

        @pl.when((t_right > c) & (t_right < C) & (c > 0))
        def _():
            merge(t_right, 0)
            rightward(t_right).start()

        @pl.when((t_left >= 0) & (t_left < c) & (c < C - 1))
        def _():
            merge(t_left, 1)
            leftward(t_left).start()

    fetch = pltpu.make_async_copy(out_part, OP, local.at[0])
    fetch.start()
    fetch.wait()

    @pl.when(c == 0)
    def _():
        for t in range(C - 1, 0, -1):
            rightward(t).start()

    @pl.when(c == C - 1)
    def _():
        for t in range(C - 1):
            leftward(t).start()

    loads[0].wait()

    def grad_slots(p):
        at = pl.ds(pl.multiple_of(p * packed, 16), packed)

        def body(j, carry):
            cols = pl.ds(pl.multiple_of(j * 512, 512), 512)
            SG[at, cols] = jnp.dot(select[at, :], G[:, cols], preferred_element_type=f32).astype(bf16)
            return carry

        lax.fori_loop(0, width // 512, body, 0)

    later = []
    for k, peer in enumerate(p_peers):
        theirs = pl.ds(pl.multiple_of(p_at[k] * packed, 16), packed)
        later.append(remote(SG.at[theirs], gbuf.at[mine], gsend.at[k], grecv.at[k], peer))
        grad_slots(p_at[k])
        later[-1].start()
    grad_slots(q)
    later.append(pltpu.make_async_copy(SG.at[mine], gbuf.at[mine], local.at[1]))
    later[-1].start()
    for step in range(1, C - 1):
        pass_on(step)

    @pl.when(c > 0)
    def _():
        remote(OP.at[0], RB.at[c], osend.at[0, c], orecv.at[0, c], left).wait_recv()

    @pl.when(c < C - 1)
    def _():
        remote(OP.at[0], RB.at[C], osend.at[1, c], orecv.at[1, c], right).wait_recv()


    def head_rows(i, carry):
        part = pl.ds(i * 32, 32)
        total = tokens[part, :].astype(f32) + OP[c, part, :].astype(f32)
        total += jnp.where(c > 0, RB[c, part, :].astype(f32), 0.0)
        total += jnp.where(c < C - 1, RB[C, part, :].astype(f32), 0.0)
        h1[part, :] = total
        unit, _ = rms_unit(total)
        normed = (unit * gain[...]).astype(bf16)
        xm[part, :] = normed
        XM[pl.ds(pl.multiple_of(c * rows + i * 32, 16), 32), :] = normed
        return carry

    lax.fori_loop(0, rows // 32, head_rows, 0)
    chunks = []
    for j in range(CHUNKS):
        piece = XM.at[own_rows, columns(width, j)]
        chunks.append(
            [remote(piece, piece, xsend.at[j, k], xrecv.at[j, k], peer) for k, peer in enumerate(z_peers)]
        )
    for copy in chunks[0]:
        copy.start()
    logits = jnp.dot(xm[...], pack[...], preferred_element_type=f32)[:, : chosen.shape[1]]
    logits = jnp.where(chosen[...] > 0.0, logits, -jnp.inf)
    power = jnp.exp(logits - jnp.max(logits, axis=-1, keepdims=True))
    gates[...] = power / jnp.sum(power, axis=-1, keepdims=True)
    WM[own_rows, :] = gates[...] * kept[...]
    row = []
    for k, peer in enumerate(z_peers):
        piece = WM.at[own_rows, :]
        row.append(remote(piece, piece, msend.at[k], mrecv.at[k], peer))
        row[-1].start()
    for line in chunks[1:]:
        for copy in line:
            copy.start()
    sent = []
    for j in range(CHUNKS):
        cols = columns(width, j)
        for copy in chunks[j]:
            copy.wait_recv()

        def slots(i, carry):
            at = pl.ds(pl.multiple_of(i * half, 16), half)
            SL[at, cols] = jnp.dot(select[at, :], XM[:, cols], preferred_element_type=f32).astype(bf16)
            return carry

        lax.fori_loop(0, 2, slots, 0)
        line = []
        for k, peer in enumerate(p_peers):
            theirs = pl.ds(pl.multiple_of(p_at[k] * packed, 16), packed)
            line.append(
                remote(SL.at[theirs, cols], buffer.at[mine, cols], bsend.at[j, k], brecv.at[j, k], peer)
            )
        line.append(pltpu.make_async_copy(SL.at[mine, cols], buffer.at[mine, cols], local.at[4 + j]))
        for copy in line:
            copy.start()
        sent.append(line)
        if j == 0:
            for copy in row:
                copy.wait_recv()
            WS[...] = jnp.zeros_like(WS)

            place_of = lax.broadcasted_iota(jnp.int32, (Q, WM.shape[1]), 0)
            expert = (place_of // F * C + c) * F + lax.rem(place_of, F)
            spread = (lax.broadcasted_iota(jnp.int32, expert.shape, 1) == expert).astype(f32)
            lines = lax.dot_general(
                spread, WM[...], (((1,), (1,)), ((), ())),
                precision=lax.Precision.HIGHEST, preferred_element_type=f32,
            )
            for p in range(Q):
                line = lax.dot_general(
                    three_parts(lines[p : p + 1, :]), select[p * packed : (p + 1) * packed, :],
                    (((1,), (1,)), ((), ())), preferred_element_type=f32,
                )
                WS[p, :, pl.ds(0, packed)] = jnp.broadcast_to(
                    jnp.sum(line, axis=0, keepdims=True), (8, packed)
                )
            scales = [
                remote(WS.at[p_at[k]], wrow.at[q], wsend.at[k], wrecv.at[k], peer)
                for k, peer in enumerate(p_peers)
            ]
            scales.append(pltpu.make_async_copy(WS.at[q], wrow.at[q], local.at[2]))
            for copy in scales:
                copy.start()
        if j == CHUNKS - 2:
            for copy in later + loads[1:]:
                copy.wait()
            reload = pltpu.make_async_copy(gbuf, SG, local.at[3])
            reload.start()
            reload.wait()

            def through_down(i, carry):
                at = pl.ds(pl.multiple_of(i * half, 16), half)
                gw[at, :] = lax.dot_general(
                    SG[at, :], WD[...], (((1,), (1,)), ((), ())), preferred_element_type=f32
                )
                return carry

            lax.fori_loop(0, 2, through_down, 0)
    for j in range(CHUNKS - 1):
        cols = columns(width, j)
        for copy in sent[j]:
            copy.wait()

        def project(i, carry):
            at = pl.ds(pl.multiple_of(i * half, 16), half)
            part = buffer[at, cols]
            one = jnp.dot(part, WG[cols, :], preferred_element_type=f32)
            two = jnp.dot(part, WU[cols, :], preferred_element_type=f32)
            gp[at, :] = one if j == 0 else gp[at, :] + one
            up[at, :] = two if j == 0 else up[at, :] + two
            return carry

        lax.fori_loop(0, 2, project, 0)
    for copy in scales:
        copy.wait()
    diagonal = lax.broadcasted_iota(jnp.int32, (packed, packed), 0) == lax.broadcasted_iota(
        jnp.int32, (packed, packed), 1
    )
    dgr[...] = jnp.zeros_like(dgr)
    cols = columns(width, CHUNKS - 1)
    inner = dup.shape[-1]
    hidden, dgp = SG.at[:, pl.ds(0, inner)], SG.at[:, pl.ds(inner, inner)]

    def saves_of(p):
        at = pl.ds(pl.multiple_of(p * packed, 16), packed)
        pairs = ((buffer, buffer_out), (hidden, hidden_out), (dgp, dgp_out), (dup, dup_out))
        return [
            pltpu.make_async_copy(src.at[at], dst.at[at], saved.at[i, p])
            for i, (src, dst) in enumerate(pairs)
        ]

    def expert_rows(p):
        at = pl.ds(pl.multiple_of(p * packed, 16), packed)
        part = buffer[at, cols]
        gate_pre = gp[at, :] + jnp.dot(part, WG[cols, :], preferred_element_type=f32)
        up_pre = up[at, :] + jnp.dot(part, WU[cols, :], preferred_element_type=f32)
        back = gw[at, :]
        scale = jnp.sum(
            jnp.where(diagonal, wrow[p, 0:1, pl.ds(0, packed)], 0.0), axis=1, keepdims=True
        )
        sigmoid = jax.nn.sigmoid(gate_pre)
        silu = gate_pre * sigmoid
        low = (silu * up_pre).astype(bf16)
        hidden[at, :] = (scale * low.astype(f32)).astype(bf16)
        dgate = jnp.sum(back * low.astype(f32), axis=-1, keepdims=True)
        line = jnp.sum(jnp.where(diagonal, dgate, 0.0), axis=0, keepdims=True)
        dgr[p, :, pl.ds(0, packed)] = jnp.broadcast_to(line, (8, packed))
        dhid = scale * back
        dgp[at, :] = (dhid * up_pre * sigmoid * (1.0 + gate_pre * (1.0 - sigmoid))).astype(bf16)
        dup[at, :] = (dhid * silu).astype(bf16)
        for copy in saves_of(p):
            copy.start()

    sent[CHUNKS - 1][Q - 1].wait()
    expert_rows(q)

    def arrival(k, carry):
        p = lax.rem(q + Q - 1 - k, Q)
        at = pl.ds(pl.multiple_of(p * packed, 16), packed)
        came = (p // F, c, lax.rem(p, F))
        remote(
            SL.at[at, cols], buffer.at[at, cols], bsend.at[CHUNKS - 1, k], brecv.at[CHUNKS - 1, k], came
        ).wait_recv()
        expert_rows(p)
        return carry

    lax.fori_loop(0, Q - 1, arrival, 0)
    for copy in sent[CHUNKS - 1][: Q - 1]:
        copy.wait_send()
    for line in chunks + [row]:
        for copy in line:
            copy.wait_send()

    @pl.when(c < C - 1)
    def _():
        def body(t, carry):
            rightward(t).wait_send()
            return carry

        lax.fori_loop(c + 1, C, body, 0)

    @pl.when(c > 0)
    def _():
        def body(t, carry):
            leftward(t).wait_send()
            return carry

        lax.fori_loop(0, c, body, 0)

    for p in range(Q):
        for copy in saves_of(p):
            copy.wait()


def dispatch(packed, out_part, G, tokens, pack, gain, chosen, kept, select, w_gate, w_up, w_down):
    S, C, F = sizes()
    Q = S * F
    rows, width = tokens.shape
    inner = w_gate.shape[-1]
    lanes = round_up(packed, 128)
    wide = chosen.shape[1]
    V = pltpu.VMEM
    sds = jax.ShapeDtypeStruct
    vm = pl.BlockSpec(memory_space=pltpu.VMEM)
    slots = Q * packed
    return pl.pallas_call(
        functools.partial(dispatch_kernel, packed),
        out_shape=[
            sds((slots, width), bf16),
            sds((slots, width), bf16),
            sds((Q, 8, lanes), f32),
            sds((rows, width), f32),
            sds((rows, width), bf16),
            sds((rows, wide), f32),
            sds((slots, inner), bf16),
            sds((slots, inner), bf16),
            sds((slots, inner), bf16),
            sds((Q, 8, lanes), f32),
        ],
        in_specs=[ANY, ANY] + [vm] * 6 + [ANY] * 3,
        out_specs=[ANY, ANY, vm, vm, vm, vm, ANY, ANY, ANY, vm],
        scratch_shapes=[
            V((C, rows, width), bf16),
            V((C + 1, rows, width), bf16),
            V((C * rows, width), bf16),
            V((slots, width), bf16),
            V((C * rows, wide), f32),
            V((Q, 8, lanes), f32),
            V((C * rows, width), bf16),
            V((slots, width), bf16),
            V((slots, width), bf16),
            V((width, inner), bf16), V((width, inner), bf16), V((inner, width), bf16),
            V((slots, inner), f32), V((slots, inner), f32), V((slots, inner), f32),
            V((slots, inner), bf16),
            DMA((4 + CHUNKS,)),
            DMA((4,)),
            DMA((4, Q)),
            DMA((2, C)), DMA((2, C)),
            DMA((Q - 1,)), DMA((Q - 1,)),
            DMA((CHUNKS, C - 1)), DMA((CHUNKS, C - 1)),
            DMA((C - 1,)), DMA((C - 1,)),
            DMA((CHUNKS, Q - 1)), DMA((CHUNKS, Q - 1)),
            DMA((Q - 1,)), DMA((Q - 1,)),
        ],
        name="dispatch_rows",
        compiler_params=params(3, 62 * 2**20),
    )(out_part, G, tokens, pack, gain, chosen, kept, select, w_gate, w_up, w_down)


def return_kernel(
    packed, experts, dgr, select, select_t, gates, pack, h1, gain, cot, xm, hidden, dgp, dup,
    w_gate, w_up, w_down,
    DA, y_part, dh1, small,
    RD, YB, PART, RX, DG, DGP, RG, DL, din, wy, WG, WU, WD, dlog, gnorm, DXR,
    local, load, dsend, drecv, gsend, grecv, ysend, yrecv, xsend, xrecv, msend, mrecv, *asems,
):
    S, C, F = sizes()
    s, c, f = place()
    Q = S * F
    q = s * F + f
    rows, width = h1.shape
    z_peers = z_neighbours()
    p_at, p_peers = plane_neighbours()
    loads = []
    for j in range(CHUNKS):
        cols = columns(width, j)
        loads.append(
            [
                pltpu.make_async_copy(w_gate.at[0, cols], WG.at[cols], load.at[0, j]),
                pltpu.make_async_copy(w_up.at[0, cols], WU.at[cols], load.at[1, j]),
            ]
        )
    load_down = pltpu.make_async_copy(w_down.at[0], WD, load.at[2, 0])
    for line in loads:
        for copy in line:
            copy.start()
    load_down.start()
    greet_all(z_peers + p_peers)
    half = halves(Q * packed)
    mine = pl.ds(pl.multiple_of(q * packed, 16), packed)
    theirs = [pl.ds(pl.multiple_of(at * packed, 16), packed) for at in p_at]
    inner_products = [
        remote(dgr.at[p_at[k]], DG.at[q], gsend.at[k], grecv.at[k], peer)
        for k, peer in enumerate(p_peers)
    ]
    inner_products.append(pltpu.make_async_copy(dgr.at[q], DG.at[q], local.at[0]))
    for copy in inner_products:
        copy.start()
    chunks = []
    for j in range(CHUNKS):
        cols = columns(width, j)
        for copy in loads[j]:
            copy.wait()

        def expert_in(i, carry):
            at = pl.ds(pl.multiple_of(i * half, 16), half)
            across = (((1,), (1,)), ((), ()))
            total = lax.dot_general(dgp[at, :], WG[cols, :], across, preferred_element_type=f32)
            total += lax.dot_general(dup[at, :], WU[cols, :], across, preferred_element_type=f32)
            din[at, cols] = total.astype(bf16)
            return carry

        lax.fori_loop(0, 2, expert_in, 0)
        line = [
            remote(din.at[theirs[k], cols], RD.at[mine, cols], dsend.at[j, k], drecv.at[j, k], peer)
            for k, peer in enumerate(p_peers)
        ]
        line.append(pltpu.make_async_copy(din.at[mine, cols], RD.at[mine, cols], local.at[2 + j]))
        for copy in line:
            copy.start()
        chunks.append(line)
    load_down.wait()
    def expert_out(i, carry):
        at = pl.ds(pl.multiple_of(i * half, 16), half)

        def body(j, carry):
            cols = pl.ds(pl.multiple_of(j * 512, 512), 512)
            y = jnp.dot(hidden[at, :], WD[:, cols], preferred_element_type=f32)
            wy[at, cols] = y.astype(bf16)
            return carry

        return lax.fori_loop(0, width // 512, body, carry)

    lax.fori_loop(0, 2, expert_out, 0)
    sums = []
    for j in range(CHUNKS):
        cols = columns(width, j)
        for copy in chunks[j]:
            copy.wait()

        def combine(i, carry):
            lanes = pl.ds(pl.multiple_of(j * (width // CHUNKS) + i * 256, 256), 256)
            PART[:, lanes] = jnp.dot(
                select_t[...], RD[:, lanes], preferred_element_type=f32
            ).astype(bf16)
            return carry

        lax.fori_loop(0, width // CHUNKS // 256, combine, 0)
        for k, peer in enumerate(z_peers):
            src = PART.at[pl.ds(pl.multiple_of(peer[1] * rows, 16), rows), cols]
            sums.append(remote(src, RX.at[k, :, cols], xsend.at[j, k], xrecv.at[j, k], peer))
            sums[-1].start()
    ys = [
        remote(wy.at[theirs[k]], YB.at[mine], ysend.at[k], yrecv.at[k], peer)
        for k, peer in enumerate(p_peers)
    ]
    ys.append(pltpu.make_async_copy(wy.at[mine], YB.at[mine], local.at[1]))
    for copy in ys:
        copy.start()
    for copy in inner_products:
        copy.wait()
    wide = gates.shape[1]
    place_of = lax.broadcasted_iota(jnp.int32, (Q, wide), 0)
    expert = (place_of // F * C + c) * F + lax.rem(place_of, F)
    spread = (lax.broadcasted_iota(jnp.int32, (Q, wide), 1) == expert).astype(f32)

    for p in range(Q):
        at = pl.ds(p * packed, packed)
        line = jnp.dot(
            three_parts(DG[p, 0:1, pl.ds(0, packed)]), select[at, :], preferred_element_type=f32
        )
        DL[pl.ds(p, 1), :] = jnp.sum(line, axis=0, keepdims=True)
    DGP[...] = lax.dot_general(
        DL[...], spread, (((0,), (0,)), ((), ())),
        precision=lax.Precision.HIGHEST, preferred_element_type=f32,
    ).reshape(DGP.shape)
    more = []
    for k, peer in enumerate(z_peers):
        more.append(remote(DGP.at[peer[1]], RG.at[k], msend.at[k], mrecv.at[k], peer))
        more[-1].start()
    for copy in more:
        copy.wait()
    total = DGP[c]
    for k in range(C - 1):
        total = total + RG[k]
    dlogits = gates[...] * (total - jnp.sum(gates[...] * total, axis=-1, keepdims=True))
    dlog[...] = dlogits.astype(bf16)
    gnorm[...] = jnp.zeros_like(gnorm)
    DXR[...] = lax.dot_general(
        dlog[...], pack[:, pl.ds(0, wide)], (((1,), (1,)), ((), ())), preferred_element_type=f32
    )
    for copy in sums:
        copy.wait()

    def head_rows(i, carry):
        part = pl.ds(i * 32, 32)
        mine_part = pl.ds(pl.multiple_of(c * rows + i * 32, 16), 32)
        dxm = PART[mine_part, :].astype(f32)
        for k in range(C - 1):
            dxm = dxm + RX[k, part, :].astype(f32)
        dxm = dxm + DXR[part, :]
        unit, factor = rms_unit(h1[part, :])
        gnorm[...] += jnp.sum(dxm * unit, axis=0, keepdims=True)
        grad = cot[part, :].astype(f32) + norm_backward(dxm, unit, factor, gain[...])
        dh1[part, :] = grad
        RX[0, part, :] = grad.astype(bf16)
        return carry

    lax.fori_loop(0, rows // 32, head_rows, 0)
    keep = pltpu.make_async_copy(RX.at[0], DA.at[c], local.at[2 + CHUNKS])
    keep.start()
    line = Line(RX.at[0], lambda at: DA.at[at], *asems)
    line.start()
    for h in range(1, C - 1):
        line.hop(h)
    square = lax.broadcasted_iota(jnp.int32, (HEAD_DIM, HEAD_DIM), 0) == lax.broadcasted_iota(
        jnp.int32, (HEAD_DIM, HEAD_DIM), 1
    )
    small[...] = jnp.zeros_like(small)

    def small_rows(i, carry):
        at = pl.ds(pl.multiple_of(i * HEAD_DIM, HEAD_DIM), HEAD_DIM)
        router_part = lax.dot_general(
            xm[:, at], dlog[...], (((0,), (0,)), ((), ())), preferred_element_type=f32
        )
        column = jnp.sum(jnp.where(square, gnorm[:, at], 0.0), axis=1, keepdims=True)
        if wide > experts:
            lane = lax.broadcasted_iota(jnp.int32, router_part.shape, 1)
            small[at, :] = jnp.where(lane == experts, column, router_part).astype(bf16)
        else:
            small[at, pl.ds(0, wide)] = router_part.astype(bf16)
            lane = lax.broadcasted_iota(jnp.int32, (HEAD_DIM, HEAD_DIM), 1)
            small[at, pl.ds(wide, HEAD_DIM)] = jnp.where(lane == 0, column, 0.0).astype(bf16)
        return carry

    lax.fori_loop(0, width // HEAD_DIM, small_rows, 0)
    for copy in ys:
        copy.wait()

    def combine_y(i, carry):
        lanes = pl.ds(pl.multiple_of(i * 256, 256), 256)
        y_part[:, lanes] = jnp.dot(
            select_t[...], YB[:, lanes], preferred_element_type=f32
        ).astype(bf16)
        return carry

    lax.fori_loop(0, width // 256, combine_y, 0)
    line.hop(C - 1)
    line.finish()
    keep.wait()


def give_back(
    packed, experts, dgr, select, select_t, gates, pack, h1, gain, cot, xm, hidden, dgp, dup, w_gate, w_up, w_down
):
    S, C, F = sizes()
    Q = S * F
    rows, width = h1.shape
    wide = gates.shape[1]
    inner = w_gate.shape[-1]
    V = pltpu.VMEM
    sds = jax.ShapeDtypeStruct
    vm = pl.BlockSpec(memory_space=pltpu.VMEM)
    return pl.pallas_call(
        functools.partial(return_kernel, packed, experts),
        out_shape=[
            sds((C, rows, width), bf16),
            sds((C * rows, width), bf16),
            sds((rows, width), f32),
            sds(pack.shape, bf16),
        ],
        in_specs=[vm] * 12 + [ANY] * 3,
        out_specs=[ANY] + [vm] * 3,
        scratch_shapes=[
            V((Q * packed, width), bf16),
            V((Q * packed, width), bf16),
            V((C * rows, width), bf16),
            V((C - 1, rows, width), bf16),
            V(dgr.shape, f32),
            V((C, rows, wide), f32),
            V((C - 1, rows, wide), f32),
            V((Q, C * rows), f32),
            V((Q * packed, width), bf16),
            V((Q * packed, width), bf16),
            V((width, inner), bf16), V((width, inner), bf16), V((inner, width), bf16),
            V((rows, wide), bf16),
            V((1, width), f32),
            V((rows, width), f32),
            DMA((3 + CHUNKS,)),
            DMA((3, CHUNKS)),
            DMA((CHUNKS, Q - 1)), DMA((CHUNKS, Q - 1)),
            DMA((Q - 1,)), DMA((Q - 1,)),
            DMA((Q - 1,)), DMA((Q - 1,)),
            DMA((CHUNKS, C - 1)), DMA((CHUNKS, C - 1)),
            DMA((C - 1,)), DMA((C - 1,)),
        ]
        + line_sems(C),
        name="return_grads",
        compiler_params=params(5, 62 * 2**20),
    )(dgr, select, select_t, gates, pack, h1, gain, cot, xm, hidden, dgp, dup, w_gate, w_up, w_down)


def backward_kernel(
    block, da, w_in, wo, q, k, v, xnt_in, x_in, cosine, sine, pos_col, pos_row, gains, go, sp, yp,
    OH, OX, Q3, KV3, S3, T3, YP, *rest,
):
    DX = rest[: lax.axis_size("ctx")]
    (
    w, xnt, x, late, dxn, dxsem, kr, dkr, dv, acc, DQ, head_grad,
        GQ, Q1, Q2, QS, o_own, o_in, s_own, s_in, s_plane, s_sum, T, t_in, t_plane, t_sum,
        local, qlocal, csend, crecv, fsend, frecv, zsend, zrecv, qcs, qcr, qfs, qfr, qzs, qzr, ysend, yrecv,
    ) = rest[lax.axis_size("ctx") :]
    S, C, F = sizes()
    s, c, f = place()
    step = pl.program_id(0)
    units = GQ.shape[0]
    pairs = units - 1
    length, width = x.shape
    wide = 2 * HEAD_DIM
    late_loads = [
        pltpu.make_async_copy(src, dst, late.at[i])
        for i, (src, dst) in enumerate(((xnt_in, xnt), (w_in, w), (x_in, x)))
    ]
    z_peers = z_neighbours()
    f_peers = [(s, c, lax.rem(f + k, F)) for k in range(1, F)]
    sibling = (1 - s, c, f)
    cols = pl.ds(pl.multiple_of(step * wide, wide), wide)

    o_first = remote(go.at[1 - s], o_in, csend.at[0], crecv.at[0], sibling)
    t_first = remote(T, t_in, csend.at[2], crecv.at[2], sibling)
    o_load = pltpu.make_async_copy(go.at[s], o_own, local.at[0])
    half = F // 2
    mine = lax.rem(f // half, 2)
    o_saves = [
        pltpu.make_async_copy(o_own.at[pl.ds(mine * half, half)], OH, local.at[2]),
        pltpu.make_async_copy(o_own.at[pl.ds((1 - mine) * half, half)], OX, local.at[6]),
    ]
    s_first = remote(sp.at[1 - s], s_in, csend.at[1], crecv.at[1], sibling)
    s_load = pltpu.make_async_copy(sp.at[s], s_own, local.at[1])
    f_at = list(enumerate(f_peers))
    z_at = list(enumerate(z_peers))
    s_second = [remote(s_own.at[:, p[2]], s_plane.at[k], fsend.at[1, k], frecv.at[1, k], p) for k, p in f_at]
    t_second = [remote(T, t_plane.at[k], fsend.at[2, k], frecv.at[2, k], p) for k, p in f_at]
    s_third = [remote(s_sum.at[p[1]], S3.at[c], zsend.at[1, k], zrecv.at[1, k], p) for k, p in z_at]
    s_third.append(pltpu.make_async_copy(s_sum.at[c], S3.at[c], local.at[3]))
    t_third = [remote(t_sum, T3.at[c], zsend.at[2, k], zrecv.at[2, k], p) for k, p in z_at]
    t_third.append(pltpu.make_async_copy(t_sum, T3.at[c], local.at[4]))
    y_copies = [remote(yp.at[p[1]], YP.at[c], ysend.at[k], yrecv.at[k], p) for k, p in z_at]
    y_copies.append(pltpu.make_async_copy(yp.at[c], YP.at[c], local.at[5]))

    def q_first(u):
        return remote(GQ.at[u, 1 - s], Q1.at[u], qcs.at[u], qcr.at[u], sibling)

    def q_second(u):
        return [remote(GQ.at[u, s, :, p[2]], Q2.at[u, k], qfs.at[u, k], qfr.at[u, k], p) for k, p in f_at]

    def q_third(u):
        if isinstance(u, int) and u == pairs:
            landing = KV3.at[c]
        else:
            landing = Q3.at[:, pl.ds(pl.multiple_of(c * pairs * wide + u * wide, wide), wide)]
        copies = [
            remote(QS.at[u, p[1]], landing, qzs.at[u, k], qzr.at[u, k], p) for k, p in z_at
        ]
        copies.append(pltpu.make_async_copy(QS.at[u, c], landing, qlocal.at[u]))
        return copies

    def to_plane(u):
        q_first(u).wait()

        def body(i, carry):
            at = (u, s, i // F, lax.rem(i, F))
            GQ[at] = (GQ[at].astype(f32) + Q1[u, i // F, lax.rem(i, F)].astype(f32)).astype(bf16)
            return carry

        lax.fori_loop(0, C * F, body, 0)
        for copy in q_second(u):
            copy.start()

    def to_ctx(u):
        for copy in q_second(u):
            copy.wait()

        def body(i, carry):
            total = GQ[u, s, i, f].astype(f32)
            for k in range(F - 1):
                total = total + Q2[u, k, i].astype(f32)
            QS[u, i] = total.astype(bf16)
            return carry

        lax.fori_loop(0, C, body, 0)
        for copy in q_third(u):
            copy.start()

    @pl.when(step == 0)
    def _():
        for copy in late_loads:
            copy.start()
        greet_all(z_peers + f_peers + [sibling])
        for copy in [s_first, s_load, o_first, o_load] + y_copies:
            copy.start()
        unit, _ = rms_unit(k[...])
        kr[...] = half_turn(unit * gains[1:2, :], cosine[...], sine[...]).astype(bf16)
        dkr[...] = jnp.zeros_like(dkr)
        dv[...] = jnp.zeros_like(dv)
        head_grad[...] = jnp.zeros_like(head_grad)
        acc[...] = jnp.zeros_like(acc)

    @pl.when(step >= 1)
    def _():
        to_plane(step - 1)

    @pl.when(step == 1)
    def _():
        o_first.wait()
        o_load.wait()

        def o_body(i, carry):
            o_own[i] = (o_own[i].astype(f32) + o_in[i].astype(f32)).astype(bf16)
            return carry

        lax.fori_loop(0, F, o_body, 0)
        for copy in o_saves:
            copy.start()
        s_first.wait()
        s_load.wait()

        def s_body(i, carry):
            at = (i // F, lax.rem(i, F))
            s_own[at] = (s_own[at].astype(f32) + s_in[at].astype(f32)).astype(bf16)
            return carry

        lax.fori_loop(0, C * F, s_body, 0)
        for copy in s_second:
            copy.start()

    @pl.when(step >= 2)
    def _():
        to_ctx(step - 2)

    @pl.when(step == 2)
    def _():
        for copy in s_second:
            copy.wait()

        def s_body(i, carry):
            total = s_own[i, f].astype(f32)
            for k in range(F - 1):
                total = total + s_plane[k, i].astype(f32)
            s_sum[i] = total.astype(bf16)
            return carry

        lax.fori_loop(0, C, s_body, 0)
        for copy in s_third:
            copy.start()

    @pl.when(step < pairs)
    def _():
        dm = lax.dot_general(
            da[...], wo[cols, :], (((1,), (1,)), ((), ())), preferred_element_type=f32
        ).astype(bf16)
        for half in range(2):
            lanes = slice(half * HEAD_DIM, (half + 1) * HEAD_DIM)
            for part in range(length // block):
                rows = slice(part * block, (part + 1) * block)
                unit, factor = rms_unit(q[rows, lanes])
                cos, sin = cosine[rows, :], sine[rows, :]
                qr = half_turn(unit * gains[0:1, :], cos, sin).astype(bf16)
                keys = kr[...]
                probs = score_block(qr, keys, pos_col[rows, :], pos_row[...])
                dmh = dm[rows, lanes]
                dprobs = lax.dot_general(
                    dmh, v[...], (((1,), (1,)), ((), ())), preferred_element_type=f32
                )
                delta = jnp.sum(probs * dprobs, axis=-1, keepdims=True)
                dscores = (probs * (dprobs - delta)).astype(bf16)
                dqr = jnp.dot(dscores, keys, preferred_element_type=f32) * (HEAD_DIM**-0.5)
                rows_in = (((0,), (0,)), ((), ()))
                dkr[...] += lax.dot_general(dscores, qr, rows_in, preferred_element_type=f32) * (
                    HEAD_DIM**-0.5
                )
                dv[...] += lax.dot_general(
                    probs.astype(bf16), dmh, rows_in, preferred_element_type=f32
                )
                dqs = half_turn(dqr, cos, -sin)
                head_grad[0:1, :] += jnp.sum(dqs * unit, axis=0, keepdims=True)
                DQ[rows, lanes] = norm_backward(dqs, unit, factor, gains[0:1, :]).astype(bf16)

    @pl.when(step == pairs)
    def _():
        unit, factor = rms_unit(k[...])
        dks = half_turn(dkr[...], cosine[...], -sine[...])
        head_grad[1:2, :] += jnp.sum(dks * unit, axis=0, keepdims=True)
        DQ[:, :HEAD_DIM] = norm_backward(dks, unit, factor, gains[1:2, :]).astype(bf16)
        DQ[:, HEAD_DIM:] = dv[...].astype(bf16)

    @pl.when(step == 0)
    def _():
        for copy in late_loads:
            copy.wait()

    def weight_rows(i, carry):
        part = F * GQ.shape[4]
        rows = pl.ds(pl.multiple_of(i * part, 16), part)
        piece = jnp.dot(xnt[rows, :], DQ[...], preferred_element_type=f32)
        GQ[step, i // C, lax.rem(i, C)] = piece.astype(bf16).reshape(GQ.shape[3:])
        return carry

    lax.fori_loop(0, S * C, weight_rows, 0)
    q_first(step).start()
    for j in range(4):
        part = pl.ds(j * (width // 4), width // 4)
        acc[:, part] += lax.dot_general(
            DQ[...], w[part, cols], (((1,), (1,)), ((), ())), preferred_element_type=f32
        )

    @pl.when(step == pairs)
    def _():
        to_ctx(pairs - 1)
        to_plane(pairs)
        rows_of = width // HEAD_DIM
        total = jnp.zeros((1, width), f32)

        def finish(i, total):
            rows = pl.ds(i * 64, 64)
            unit, _ = rms_unit(x[rows, :].astype(f32))
            term = acc[rows, :]
            dxn[rows, :] = term.astype(bf16)
            return total + jnp.sum(term * unit, axis=0, keepdims=True)

        total = lax.fori_loop(0, length // 64, finish, total)
        rows = length // C
        x_saves = [
            pltpu.make_async_copy(
                dxn.at[pl.ds(pl.multiple_of(lax.rem(c + i, C) * rows, 16), rows)], DX[i], dxsem.at[i]
            )
            for i in range(C)
        ]
        for copy in x_saves:
            copy.start()
        for r in range(rows_of):
            T[r : r + 1, :] = total[:, r * HEAD_DIM : (r + 1) * HEAD_DIM]
        T[rows_of:, :] = head_grad[...]
        t_first.start()
        t_first.wait()
        T[...] = T[...] + t_in[...]
        for copy in t_second:
            copy.start()
        to_ctx(pairs)
        for copy in t_second:
            copy.wait()
        order = []
        for g in range(F):
            term = jnp.zeros_like(T)
            for k in range(F - 1):
                came = lax.rem(f + F - (k + 1), F)
                term = term + jnp.where(came == g, t_plane[k], 0.0)
            order.append(term + jnp.where(f == g, T[...], 0.0))
        total = order[0]
        for term in order[1:]:
            total = total + term
        t_sum[...] = total
        for copy in t_third:
            copy.start()
        for copy in s_third + y_copies + o_saves + t_third + x_saves:
            copy.wait()
        for u in range(units):
            for copy in q_third(u):
                copy.wait()


def backward(da, w, wo, q, k, v, xnt, x, cosine, sine, pos_col, pos_row, gains, go, sp, yp):
    S, C, F = sizes()
    length, width = x.shape
    head_width = wo.shape[0]
    pairs = head_width // (2 * HEAD_DIM)
    units = pairs + 1
    shard = sp.shape[3]
    block = min(length, 512)
    wide = 2 * HEAD_DIM
    once = pl.Buffered(buffer_count=1)
    whole = lambda array: pl.BlockSpec(array.shape, lambda i: (0, 0), pipeline_mode=once)
    sds = jax.ShapeDtypeStruct
    V = pltpu.VMEM
    q_block, o_block, s_block = (shard, wide), go.shape[2:], sp.shape[3:]
    t_block = (width // HEAD_DIM + 8, HEAD_DIM)
    return pl.pallas_call(
        functools.partial(backward_kernel, block),
        out_shape=[
            sds((F // 2,) + o_block, bf16),
            sds((F // 2,) + o_block, bf16),
            sds((shard, C * head_width), bf16),
            sds((C, shard, wide), bf16),
            sds((C,) + s_block, bf16),
            sds((C,) + t_block, f32),
            sds(yp.shape, bf16),
        ]
        + [sds((length // C, width), bf16)] * C,
        grid=(units,),
        in_specs=[whole(da), ANY, whole(wo)]
        + [pl.BlockSpec((length, wide), lambda i: (0, jnp.minimum(i, pairs - 1)))]
        + [whole(k), whole(v), ANY, ANY]
        + [whole(array) for array in (cosine, sine, pos_col, pos_row, gains)]
        + [ANY] * 3,
        out_specs=[ANY] * (7 + C),
        scratch_shapes=[
            V(w.shape, bf16), V(xnt.shape, bf16), V(x.shape, bf16), DMA((3,)),
            V((length, width), bf16), DMA((C,)),
            V((length, HEAD_DIM), bf16), V((length, HEAD_DIM), f32), V((length, HEAD_DIM), f32),
            V((length, width), f32), V((length, wide), bf16), V((8, HEAD_DIM), f32),
            V((units, S, C, F) + q_block, bf16), V((units, C, F) + q_block, bf16),
            V((units, F - 1, C) + q_block, bf16), V((units, C) + q_block, bf16),
            V((F,) + o_block, bf16), V((F,) + o_block, bf16),
            V((C, F) + s_block, bf16), V((C, F) + s_block, bf16), V((F - 1, C) + s_block, bf16), V((C,) + s_block, bf16),
            V(t_block, f32), V(t_block, f32), V((F - 1,) + t_block, f32), V(t_block, f32),
            DMA((7,)), DMA((units,)),
            DMA((3,)), DMA((3,)), DMA((3, F - 1)), DMA((3, F - 1)), DMA((3, C - 1)), DMA((3, C - 1)),
            DMA((units,)), DMA((units,)), DMA((units, F - 1)), DMA((units, F - 1)),
            DMA((units, C - 1)), DMA((units, C - 1)), DMA((C - 1,)), DMA((C - 1,)),
        ],
        name="attention_backward",
        compiler_params=params(7, 60 * 2**20),
    )(da, w, wo, q, k, v, xnt, x, cosine, sine, pos_col, pos_row, gains, go, sp, yp)


def dot(left, right):
    return jnp.dot(left, right, preferred_element_type=f32)


def contract_rows(left, right):
    return lax.dot_general(left, right, (((0,), (0,)), ((), ())), preferred_element_type=f32)


def times_transpose(left, right):
    return lax.dot_general(left, right, (((1,), (1,)), ((), ())), preferred_element_type=f32)


def on_device(
    tokens,
    stretch_order,
    expert_ids,
    slot_index,
    norm_attn,
    head_gains,
    w_query,
    w_key,
    w_value,
    w_out,
    norm_moe,
    w_router,
    w_gate,
    w_up,
    w_down,
    cotangent,
):
    S, C, F = sizes()
    Q = S * F
    seq_at, ctx_at, fsdp_at = place()
    rows, width = tokens.shape[1:]
    length = C * rows
    experts = w_router.shape[1]
    capacity = rows * TOP // (Q * C) + 1
    packed = round_up(C * capacity, 16)
    lanes = round_up(packed, 128)
    head_width = w_query.shape[1] // C
    shard = w_router.shape[0]
    pack_width = round_up(experts + 2, 128)
    (
        X, W, WO, PK, _, G, out_part, q, k, v, mixed, xnt, gain_attn, gain_moe, gains,
        cosine, sine, pos_col, pos_row, select, select_t, chosen, kept_map,
    ) = front(
        capacity, packed, stretch_order, expert_ids[0].T, slot_index[0].T,
        tokens[0], w_query, w_key, w_value, w_out, w_router.T, norm_attn[None], norm_moe[None],
        cotangent[0], head_gains,
    )
    W = W.reshape(width, head_width + 2 * HEAD_DIM)
    WO = WO.reshape(head_width, width)
    PK = PK.reshape(width, pack_width)
    buffer, slot_grad, _, h1, xm, gates, hidden, dgp, dup, slot_dgate = dispatch(
        packed, out_part.reshape(C, rows, width), G.reshape(length, width), tokens[0], PK, gain_moe,
        chosen, kept_map, select, w_gate, w_up, w_down,
    )
    DA, y_part, dh1, small = give_back(
        packed, experts, slot_dgate, select, select_t, gates, PK, h1, gain_moe, cotangent[0],
        xm, hidden, dgp, dup, w_gate, w_up, w_down,
    )
    DA = DA.reshape(length, width)
    grad_out_part = contract_rows(mixed, DA).astype(bf16)
    out_parts = grad_out_part.reshape(S, F, head_width // Q, width)

    def part_of(parts, at):
        return lax.dynamic_index_in_dim(parts, at, 0, keepdims=False)

    out_half, out_other, query_sum, kv_sums, small_sums, tiny_sums, y_parts, *dxn_parts = backward(
        DA, W, WO, q, k, v, xnt, X, cosine, sine, pos_col, pos_row, gains,
        out_parts,
        small.reshape(S, C, F, shard, pack_width),
        y_part.reshape(C, rows, width),
    )
    dxn = dxn_parts[0].astype(f32)
    for i in range(1, C):
        dxn += lax.ppermute(dxn_parts[i], "ctx", [(j, (j + i) % C) for j in range(C)]).astype(f32)
    out_sum, bit = out_half, F // 2
    while True:
        came = lax.ppermute(out_other, "fsdp", [(i, i ^ bit) for i in range(F)])
        out_sum = (out_sum.astype(f32) + came.astype(f32)).astype(bf16)
        bit //= 2
        if not bit:
            break
        mine = lax.rem(fsdp_at // bit, 2)
        parts = out_sum.reshape((2, bit) + out_sum.shape[1:])
        out_sum, out_other = part_of(parts, mine), part_of(parts, 1 - mine)
    out_sum = out_sum[0]
    turn = [(i * C + j, j * S + i) for i in range(S) for j in range(C)]
    o_sum = lax.ppermute(out_sum, ("seq", "ctx"), turn)
    grad_wgate = contract_rows(buffer, dgp)
    grad_wup = contract_rows(buffer, dup)
    grad_wdown = contract_rows(hidden, slot_grad)
    layer_out = (h1 + jnp.sum(y_parts.astype(f32), axis=0)).astype(bf16)
    unit, factor = rms_unit(tokens[0].astype(f32))
    grad_tokens = (dh1 + norm_backward(dxn, unit, factor, gain_attn)).astype(bf16)
    grad_query = query_sum.astype(f32)

    def key_columns(block):
        pieces = block.astype(f32).reshape(KEY_VALUE_HEADS, C // KEY_VALUE_HEADS, shard, HEAD_DIM).sum(axis=1)
        return pieces.transpose(1, 0, 2).reshape(shard, KEY_VALUE_HEADS * HEAD_DIM)

    grad_key = key_columns(kv_sums[:, :, :HEAD_DIM])
    grad_value = key_columns(kv_sums[:, :, HEAD_DIM:])
    small_sum = jnp.sum(small_sums.astype(f32), axis=0)
    tiny_sum = jnp.sum(tiny_sums, axis=0)
    tiny_rows = width // HEAD_DIM
    device = (seq_at * C + ctx_at) * F + fsdp_at
    grad_norm_attn = lax.dynamic_slice_in_dim(
        tiny_sum[:tiny_rows].reshape(width), device * shard, shard
    )
    return (
        layer_out[None],
        grad_tokens[None],
        grad_norm_attn,
        tiny_sum[tiny_rows : tiny_rows + 2],
        grad_query,
        grad_key,
        grad_value,
        o_sum.astype(f32),
        small_sum[:, experts],
        small_sum[:, :experts],
        grad_wgate[None],
        grad_wup[None],
        grad_wdown[None],
    )


def solution(mesh):
    rows = P(("seq", "fsdp"), "ctx", None)
    vector = P(AXES)
    matrix = P(AXES, None)
    cube = P(AXES, None, None)
    return jax.shard_map(
        on_device,
        mesh=mesh,
        in_specs=(
            rows, P(), rows, rows, vector, P(), matrix, matrix, matrix, matrix,
            vector, matrix, cube, cube, cube, rows,
        ),
        out_specs=(
            rows, rows, vector, P(), matrix, matrix, matrix, matrix, vector, matrix,
            cube, cube, cube,
        ),
        check_vma=False,
    )
```

profile of v0, /device:TPU:1, one launch (start us, length us, event | category | flops | bytes accessed | tf_op | source)
XLA Modules:
  0.0 496.9 jit_solution(6424889610194271943)
XLA Ops:
  0.6 105.2 %gather_and_attend.1 = (bf16[512,2048]{1,0:T(8,128)(2,1)}, bf16[2,4,4,64,1280]{4,3,2,1,0:T(8,128)(2,1)}, bf16[2,4,128,2048]{3,2,1,0:T(8,128)(2,1)}, bf16[2,4,4,6...) custom-call(s32[8]{0:T(128)} %order.1, ...), custom_call_target="tpu_custom_call" | custom-call | tf_op jit(solution)/shard_map/gather_and_attend/pallas_call | solution.py:462
  105.9 121.1 %dispatch_rows.1 = (bf16[1152,2048]{1,0:T(8,128)(2,1)}, bf16[1152,2048]{1,0:T(8,128)(2,1)}, f32[8,8,256]{2,1,0:T(8,128)}, f32[128,2048]{1,0:T(8,128)}, bf16[128,...) custom-call(bf16[4,128,2048]{2,1,0:T(8,128)(2,1)} %bitcast.63, ...), custom_call_target="tpu_custom_call" | custom-call | tf_op jit(solution)/shard_map/dispatch_rows/pallas_call | solution.py:849
  227.0 127.4 %return_grads.1 = (bf16[4,128,2048]{2,1,0:T(8,128)(2,1)}, bf16[512,2048]{1,0:T(8,128)(2,1)}, f32[128,2048]{1,0:T(8,128)}, bf16[2048,128]{1,0:T(8,128)(2,1)}) custom-call(f32[8,8,256]{2,1,0:T(8,128)} %get-tuple-element.67.dgr, bf16[1152,512]{1,0:T(8,128)(2,1)} %get-tuple-element.65.select, bf16[512,1152]{1,0:T(8,128)(2,1)} %get-tuple-element.68.select_t, ...), custom_call_target="tpu_custom_call" | custom-call | tf_op jit(solution)/shard_map/return_grads/pallas_call | solution.py:1097
  354.4 6.0 %convolution_convert_fusion = bf16[1024,2048]{1,0:T(8,128)(2,1)} fusion(bf16[512,1024]{1,0:T(8,128)(2,1)S(1)} %copy-done.12, bf16[512,2048]{1,0:T(8,128)(2,1)} %bitcast.68), kind=kOutput, calls=%fused_computation.1 | convolution fusion | flops 2149580800 | bytes 7340032 | tf_op jit(solution)/shard_map/dot_general | solution.py:1464
  360.4 69.2 %attention_backward.1 = (bf16[2,128,2048]{2,1,0:T(8,128)(2,1)}, bf16[2,128,2048]{2,1,0:T(8,128)(2,1)}, bf16[64,4096]{1,0:T(8,128)(2,1)}, bf16[4,64,256]{2,1,0:T(...) custom-call(bf16[512,2048]{1,0:T(8,128)(2,1)} %bitcast.69, ...), custom_call_target="tpu_custom_call" | custom-call | tf_op jit(solution)/shard_map/attention_backward/pallas_call | solution.py:1420
  429.7 0.9 collective-permute-start
  431.3 1.7 collective-permute-start.2
  433.0 1.4 collective-permute-start.3
  434.6 8.7 %convolution_bitcast_fusion.1 = f32[1,2048,768]{2,1,0:T(8,128)} fusion(bf16[1152,2048]{1,0:T(8,128)(2,1)} %get-tuple-element.103, bf16[1152,768]{1,0:T(8,128)(2,1)S(1)} %copy-done.6), kind=kOutput, calls=%fused_computation.3 | convolution fusion | flops 3623878656 | bytes 12779520 | tf_op jit(solution)/shard_map/dot_general | solution.py:1464
  443.3 6.3 %convolution_bitcast_fusion.2 = f32[1,2048,768]{2,1,0:T(8,128)} fusion(bf16[1152,2048]{1,0:T(8,128)(2,1)S(1)} %bitcast.81, bf16[1152,768]{1,0:T(8,128)(2,1)S(1)} %copy-done.5), kind=kOutput, calls=%fused_computation.4 | convolution fusion | flops 3623878656 | bytes 12779520 | tf_op jit(solution)/shard_map/dot_general | solution.py:1464
  450.9 0.9 fusion.8
  454.0 8.6 %convolution_bitcast_fusion = f32[1,768,2048]{2,1,0:T(8,128)} fusion(bf16[1152,768]{1,0:T(8,128)(2,1)S(1)} %copy-done.4, bf16[1152,2048]{1,0:T(8,128)(2,1)} %get-tuple-element.104), kind=kOutput, calls=%fused_computation.2 | convolution fusion | flops 3623878656 | bytes 12779520 | tf_op jit(solution)/shard_map/dot_general | solution.py:1464
  462.6 1.6 add_convert_fusion
  464.2 0.8 constant_dynamic-slice_fusion
  465.1 1.1 collective-permute-start.4
  468.1 2.1 convert_element_type.67
  470.2 1.3 dynamic_slice.6
  471.5 1.6 fusion.2
  473.1 3.1 collective-permute-done.4
  476.2 1.2 fusion.9
  477.4 7.4 %collective-permute-start.5 = (bf16[128,2048]{1,0:T(8,128)(2,1)S(1)}, bf16[128,2048]{1,0:T(8,128)(2,1)S(1)}, u32[]{:S(2)}, u32[]{:S(2)}) collective-permute-start(bf16[128,2048]{1,0:T(8,128)(2,1)S(1)} %fusion.9), channel_id=1, source_target_pairs={{0,0},{4,8},{8,16},{12,24},{16,4},{20,12},{24,20},{28,28},{1,1},{5... | collective-permute-start | bytes 1572872 | tf_op jit(solution)/shard_map/ppermute | solution.py:1548
  484.8 2.5 fusion.10
  487.2 8.4 %collective-permute-done.5 = bf16[128,2048]{1,0:T(8,128)(2,1)S(1)} collective-permute-done((bf16[128,2048]{1,0:T(8,128)(2,1)S(1)}, bf16[128,2048]{1,0:T(8,128)(2,1)S(1)}, u32[]{:S(2)}, u32[]{:S(2)}) %collective-permute-start.5) | collective-permute-done | bytes 524320 | tf_op jit(solution)/shard_map/ppermute | solution.py:1548
  495.6 1.1 convert_element_type.74
  (48 shorter events, 6.3 us)
Async XLA Ops:
  227.0 127.5 %copy-start.12 = (bf16[512,1024]{1,0:T(8,128)(2,1)S(1)}, bf16[512,1024]{1,0:T(8,128)(2,1)}, u32[]{:S(2)}) copy-start(bf16[512,1024]{1,0:T(8,128)(2,1)} %get-tuple-element.87) | copy-start | bytes 3145732
  360.4 73.9 %copy-start = (bf16[1,128,2048]{2,1,0:T(8,128)(2,1)S(1)}, bf16[1,128,2048]{2,1,0:T(8,128)(2,1)}, u32[]{:S(2)}) copy-start(bf16[1,128,2048]{2,1,0:T(8,128)(2,1)} %param.17) | copy-start | bytes 1572868
  360.4 74.1 %copy-start.6 = (bf16[1152,768]{1,0:T(8,128)(2,1)S(1)}, bf16[1152,768]{1,0:T(8,128)(2,1)}, u32[]{:S(2)}) copy-start(bf16[1152,768]{1,0:T(8,128)(2,1)} %get-tuple-element.73.dup) | copy-start | bytes 5308420
  360.4 82.9 %slice-start = ((s8[4718592]{0:T(1024)(128)(4,1)}), s8[524288]{0:T(1024)(128)(4,1)S(1)}, s32[]{:S(2)}) async-start(s8[4718592]{0:T(1024)(128)(4,1)} %bitcast.80), calls=%async_computation | async-start | bytes 1048576
  429.7 41.8 %collective-permute-start = (bf16[128,2048]{1,0:T(8,128)(2,1)}, bf16[128,2048]{1,0:T(8,128)(2,1)S(1)}, u32[]{:S(2)}, u32[]{:S(2)}) collective-permute-start(bf16[128,2048]{1,0:T(8,128)(2,1)} %get-tuple-element.93), channel_id=1, source_target_pairs={{0,4},{4,8},{8,12},{12,0},{1,5},{5,9},{9,13},{13,1},{2,6},{6,10},{... | collective-permute-start | bytes 1572872 | tf_op jit(solution)/shard_map/ppermute | solution.py:1535
  430.5 40.9 %collective-permute-start.1 = (bf16[128,2048]{1,0:T(8,128)(2,1)}, bf16[128,2048]{1,0:T(8,128)(2,1)S(1)}, u32[]{:S(2)}, u32[]{:S(2)}) collective-permute-start(bf16[128,2048]{1,0:T(8,128)(2,1)} %get-tuple-element.94), channel_id=1, source_target_pairs={{0,8},{4,12},{8,0},{12,4},{1,9},{5,13},{9,1},{13,5},{2,10},{6,14},... | collective-permute-start | bytes 1572872 | tf_op jit(solution)/shard_map/ppermute | solution.py:1535
  431.3 40.2 %collective-permute-start.2 = (bf16[128,2048]{1,0:T(8,128)(2,1)}, bf16[128,2048]{1,0:T(8,128)(2,1)}, u32[]{:S(2)}, u32[]{:S(2)}) collective-permute-start(bf16[128,2048]{1,0:T(8,128)(2,1)} %get-tuple-element.95), channel_id=1, source_target_pairs={{0,12},{4,0},{8,4},{12,8},{1,13},{5,1},{9,5},{13,9},{2,14},{6,2},{... | collective-permute-start | bytes 1572872 | tf_op jit(solution)/shard_map/ppermute | solution.py:1535
  433.0 29.6 %collective-permute-start.3 = (bf16[2,128,2048]{2,1,0:T(8,128)(2,1)}, bf16[2,128,2048]{2,1,0:T(8,128)(2,1)}, u32[]{:S(2)}, u32[]{:S(2)}) collective-permute-start(bf16[2,128,2048]{2,1,0:T(8,128)(2,1)} %get-tuple-element.101), channel_id=1, source_target_pairs={{0,2},{1,3},{2,0},{3,1},{4,6},{5,7},{6,4},{7,5},{8,10},{9,11},{10,... | collective-permute-start | bytes 3145736 | tf_op jit(solution)/shard_map/ppermute | solution.py:1538
  434.6 8.8 %copy-start.5 = (bf16[1152,768]{1,0:T(8,128)(2,1)S(1)}, bf16[1152,768]{1,0:T(8,128)(2,1)}, u32[]{:S(2)}) copy-start(bf16[1152,768]{1,0:T(8,128)(2,1)} %get-tuple-element.72.dgp) | copy-start | bytes 5308420
  434.6 8.8 %slice-start.1 = ((s8[4718592]{0:T(1024)(128)(4,1)}), s8[4194304]{0:T(1024)(128)(4,1)S(1)}, s32[]{:S(2)}) async-start(s8[4718592]{0:T(1024)(128)(4,1)} %bitcast.80), calls=%async_computation.1 | async-start | bytes 8388608
  443.3 6.3 %copy-start.3 = (bf16[4,128,2048]{2,1,0:T(8,128)(2,1)S(1)}, bf16[4,128,2048]{2,1,0:T(8,128)(2,1)}, u32[]{:S(2)}) copy-start(bf16[4,128,2048]{2,1,0:T(8,128)(2,1)} %get-tuple-element.90) | copy-start | bytes 6291460
  449.6 1.2 copy-start.1
  450.9 2.3 copy-start.9
  450.9 3.1 copy-start.10
  450.9 3.1 copy-start.4
  454.0 8.6 %copy-start.8 = (bf16[2,128,2048]{2,1,0:T(8,128)(2,1)S(1)}, bf16[2,128,2048]{2,1,0:T(8,128)(2,1)}, u32[]{:S(2)}) copy-start(bf16[2,128,2048]{2,1,0:T(8,128)(2,1)} %get-tuple-element.100) | copy-start | bytes 3145732
  464.2 7.2 %copy-start.2 = (bf16[128,2048]{1,0:T(8,128)(2,1)S(1)}, bf16[128,2048]{1,0:T(8,128)(2,1)}, u32[]{:S(2)}) copy-start(bf16[128,2048]{1,0:T(8,128)(2,1)} %get-tuple-element.92) | copy-start | bytes 1572868
  464.2 7.2 %copy-start.11 = (f32[1,2048]{1,0:T(1,128)S(1)}, f32[1,2048]{1,0:T(1,128)}, u32[]{:S(2)}) copy-start(f32[1,2048]{1,0:T(1,128)} %get-tuple-element.96) | copy-start | bytes 24580
  465.1 11.1 %collective-permute-start.4 = (bf16[1,128,2048]{2,1,0:T(8,128)(2,1)}, bf16[1,128,2048]{2,1,0:T(8,128)(2,1)}, u32[]{:S(2)}, u32[]{:S(2)}) collective-permute-start(bf16[1,128,2048]{2,1,0:T(8,128)(2,1)} %constant_dynamic-slice_fusion), channel_id=1, source_target_pairs={{0,1},{1,0},{2,3},{3,2},{4,5},{5,4},{6,7},{7,6},{8,9},{9,8},{10,11... | collective-permute-start | bytes 1572872 | tf_op jit(solution)/shard_map/ppermute | solution.py:1538
  471.5 13.3 %copy-start.7 = (f32[128,2048]{1,0:T(8,128)S(1)}, f32[128,2048]{1,0:T(8,128)}, u32[]{:S(2)}) copy-start(f32[128,2048]{1,0:T(8,128)} %get-tuple-element.91) | copy-start | bytes 3145732
  477.4 18.3 %collective-permute-start.5 = (bf16[128,2048]{1,0:T(8,128)(2,1)S(1)}, bf16[128,2048]{1,0:T(8,128)(2,1)S(1)}, u32[]{:S(2)}, u32[]{:S(2)}) collective-permute-start(bf16[128,2048]{1,0:T(8,128)(2,1)S(1)} %fusion.9), channel_id=1, source_target_pairs={{0,0},{4,8},{8,16},{12,24},{16,4},{20,12},{24,20},{28,28},{1,1},{5... | collective-permute-start | bytes 1572872 | tf_op jit(solution)/shard_map/ppermute | solution.py:1548
where the time goes:
time: 501 us; the launch traced here: 497 us
  Pallas kernels  423 us (84%)
  matrix products  29.6 us (6%)
  starting transfers between devices  13.2 us (3%)
  other arithmetic  12.3 us (2%)
  waiting for transfers between devices  11.5 us (2%)
  local copies, waits for them, and re-layouts  6.26 us (1%)
    pallas_call x1, Pallas kernels, give_back(): pl.pallas_call(functools.partial(return_kernel, packed, experts), out_sha...  127 us
    pallas_call x1, Pallas kernels, dispatch(): pl.pallas_call(functools.partial(dispatch_kernel, packed), out_shape=[sds...  121 us
    pallas_call x1, Pallas kernels, front(): pl.pallas_call(functools.partial(front_kernel, block, capacity, packed, e...  105 us
    pallas_call x1, Pallas kernels, backward(): pl.pallas_call(functools.partial(backward_kernel, block), out_shape=[sds(...  69.2 us
    dot_general x4, matrix products, contract_rows(): lax.dot_general(left, right, (((0,), (0,)), ((), ())), preferred_element_...  29.6 us
  transfers between devices with their start and end apart: 6, of which 2 were waited for; matrix products, arithmetic and copies ran while one was open for 8% of the time, Pallas kernels for 0%

commit v1 on v0

--- a/solution.py
+++ b/solution.py
@@ -891,10 +891,10 @@
 
 
 def return_kernel(
-    packed, experts, dgr, select, select_t, gates, pack, h1, gain, cot, xm, hidden, dgp, dup,
-    w_gate, w_up, w_down,
+    packed, experts, dgr, gates, pack, h1, gain, cot, xm, dgp, dup,
+    select_in, select_t_in, hidden_in, w_gate, w_up, w_down,
     DA, y_part, dh1, small,
-    RD, YB, PART, RX, DG, DGP, RG, DL, din, wy, WG, WU, WD, dlog, gnorm, DXR,
+    RD, YB, PART, RX, DG, DGP, RG, DL, din, wy, WG, WU, WD, dlog, gnorm, DXR, select, select_t, hidden,
     local, load, dsend, drecv, gsend, grecv, ysend, yrecv, xsend, xrecv, msend, mrecv, *asems,
 ):
     S, C, F = sizes()
@@ -914,10 +914,17 @@
             ]
         )
     load_down = pltpu.make_async_copy(w_down.at[0], WD, load.at[2, 0])
+    late = [
+        pltpu.make_async_copy(hidden_in, hidden, load.at[2, 1]),
+        pltpu.make_async_copy(select_t_in, select_t, load.at[2, 2]),
+        pltpu.make_async_copy(select_in, select, load.at[2, 3]),
+    ]
     for line in loads:
         for copy in line:
             copy.start()
     load_down.start()
+    for copy in late:
+        copy.start()
     greet_all(z_peers + p_peers)
     half = halves(Q * packed)
     mine = pl.ds(pl.multiple_of(q * packed, 16), packed)
@@ -953,6 +960,8 @@
             copy.start()
         chunks.append(line)
     load_down.wait()
+    for copy in late:
+        copy.wait()
     def expert_out(i, carry):
         at = pl.ds(pl.multiple_of(i * half, 16), half)
 
@@ -967,6 +976,18 @@
     lax.fori_loop(0, 2, expert_out, 0)
     sums = []
     for j in range(CHUNKS):
+        if j == CHUNKS - 1:
+            ys = []
+            for jj in range(2):
+                cols = pl.ds(jj * (width // 2), width // 2)
+                line = [
+                    remote(wy.at[theirs[k], cols], YB.at[mine, cols], ysend.at[jj, k], yrecv.at[jj, k], peer)
+                    for k, peer in enumerate(p_peers)
+                ]
+                line.append(pltpu.make_async_copy(wy.at[mine, cols], YB.at[mine, cols], local.at[(1, 2 + CHUNKS + 1)[jj]]))
+                for copy in line:
+                    copy.start()
+                ys.append(line)
         cols = columns(width, j)
         for copy in chunks[j]:
             copy.wait()
@@ -983,13 +1004,6 @@
             src = PART.at[pl.ds(pl.multiple_of(peer[1] * rows, 16), rows), cols]
             sums.append(remote(src, RX.at[k, :, cols], xsend.at[j, k], xrecv.at[j, k], peer))
             sums[-1].start()
-    ys = [
-        remote(wy.at[theirs[k]], YB.at[mine], ysend.at[k], yrecv.at[k], peer)
-        for k, peer in enumerate(p_peers)
-    ]
-    ys.append(pltpu.make_async_copy(wy.at[mine], YB.at[mine], local.at[1]))
-    for copy in ys:
-        copy.start()
     for copy in inner_products:
         copy.wait()
     wide = gates.shape[1]
@@ -1067,8 +1081,6 @@
         return carry
 
     lax.fori_loop(0, width // HEAD_DIM, small_rows, 0)
-    for copy in ys:
-        copy.wait()
 
     def combine_y(i, carry):
         lanes = pl.ds(pl.multiple_of(i * 256, 256), 256)
@@ -1077,7 +1089,10 @@
         ).astype(bf16)
         return carry
 
-    lax.fori_loop(0, width // 256, combine_y, 0)
+    for j in range(2):
+        for copy in ys[j]:
+            copy.wait()
+        lax.fori_loop(j * (width // 512), (j + 1) * (width // 512), combine_y, 0)
     line.hop(C - 1)
     line.finish()
     keep.wait()
@@ -1102,7 +1117,7 @@
             sds((rows, width), f32),
             sds(pack.shape, bf16),
         ],
-        in_specs=[vm] * 12 + [ANY] * 3,
+        in_specs=[vm] * 9 + [ANY] * 6,
         out_specs=[ANY] + [vm] * 3,
         scratch_shapes=[
             V((Q * packed, width), bf16),
@@ -1119,18 +1134,19 @@
             V((rows, wide), bf16),
             V((1, width), f32),
             V((rows, width), f32),
-            DMA((3 + CHUNKS,)),
+            V(select.shape, bf16), V(select_t.shape, bf16), V(hidden.shape, bf16),
+            DMA((4 + CHUNKS,)),
             DMA((3, CHUNKS)),
             DMA((CHUNKS, Q - 1)), DMA((CHUNKS, Q - 1)),
             DMA((Q - 1,)), DMA((Q - 1,)),
-            DMA((Q - 1,)), DMA((Q - 1,)),
+            DMA((2, Q - 1)), DMA((2, Q - 1)),
             DMA((CHUNKS, C - 1)), DMA((CHUNKS, C - 1)),
             DMA((C - 1,)), DMA((C - 1,)),
         ]
         + line_sems(C),
         name="return_grads",
         compiler_params=params(5, 62 * 2**20),
-    )(dgr, select, select_t, gates, pack, h1, gain, cot, xm, hidden, dgp, dup, w_gate, w_up, w_down)
+    )(dgr, gates, pack, h1, gain, cot, xm, dgp, dup, select, select_t, hidden, w_gate, w_up, w_down)
 
 
 def backward_kernel(

time: 501 us -> 495 us (0.988)
  Pallas kernels: 423 us -> 417 us
    pallas_call x1, Pallas kernels: 127 us -> 121 us  [give_back(): pl.pallas_call(functools.partial(return_kernel, packed, experts), out_sha...]
where the time goes in v1:
time: 495 us; the launch traced here: 492 us
  Pallas kernels  417 us (84%)
  matrix products  29.6 us (6%)
  starting transfers between devices  13 us (3%)
  waiting for transfers between devices  12.9 us (3%)
  other arithmetic  12.3 us (2%)
  local copies, waits for them, and re-layouts  6.26 us (1%)
    pallas_call x1, Pallas kernels, dispatch(): pl.pallas_call(functools.partial(dispatch_kernel, packed), out_shape=[sds...  121 us
    pallas_call x1, Pallas kernels, give_back(): pl.pallas_call(functools.partial(return_kernel, packed, experts), out_sha...  121 us
    pallas_call x1, Pallas kernels, front(): pl.pallas_call(functools.partial(front_kernel, block, capacity, packed, e...  105 us
    pallas_call x1, Pallas kernels, backward(): pl.pallas_call(functools.partial(backward_kernel, block), out_shape=[sds(...  69.8 us
    dot_general x4, matrix products, contract_rows(): lax.dot_general(left, right, (((0,), (0,)), ((), ())), preferred_element_...  29.6 us
  transfers between devices with their start and end apart: 6, of which 2 were waited for; matrix products, arithmetic and copies ran while one was open for 8% of the time, Pallas kernels for 0%

profile of v1, /device:TPU:1, one launch (start us, length us, event | category | flops | bytes accessed | tf_op | source)
XLA Modules:
  0.0 491.8 jit_solution(1990355951534107206)
XLA Ops:
  0.6 105.2 %gather_and_attend.1 = (bf16[512,2048]{1,0:T(8,128)(2,1)}, bf16[2,4,4,64,1280]{4,3,2,1,0:T(8,128)(2,1)}, bf16[2,4,128,2048]{3,2,1,0:T(8,128)(2,1)}, bf16[2,4,4,6...) custom-call(s32[8]{0:T(128)} %order.1, ...), custom_call_target="tpu_custom_call" | custom-call | tf_op jit(solution)/shard_map/gather_and_attend/pallas_call | solution.py:462
  105.9 121.1 %dispatch_rows.1 = (bf16[1152,2048]{1,0:T(8,128)(2,1)}, bf16[1152,2048]{1,0:T(8,128)(2,1)}, f32[8,8,256]{2,1,0:T(8,128)}, f32[128,2048]{1,0:T(8,128)}, bf16[128,...) custom-call(bf16[4,128,2048]{2,1,0:T(8,128)(2,1)} %bitcast.63, ...), custom_call_target="tpu_custom_call" | custom-call | tf_op jit(solution)/shard_map/dispatch_rows/pallas_call | solution.py:849
  227.0 120.5 %return_grads.1 = (bf16[4,128,2048]{2,1,0:T(8,128)(2,1)}, bf16[512,2048]{1,0:T(8,128)(2,1)}, f32[128,2048]{1,0:T(8,128)}, bf16[2048,128]{1,0:T(8,128)(2,1)}) custom-call(f32[8,8,256]{2,1,0:T(8,128)} %get-tuple-element.67.dgr, f32[128,128]{1,0:T(8,128)} %get-tuple-element.68.gates, bf16[2048,128]{1,0:T(8,128)(2,1)} %bitcast.65, ...), custom_call_target="tpu_custom_call" | custom-call | tf_op jit(solution)/shard_map/return_grads/pallas_call | solution.py:1112
  347.5 6.0 %convolution_convert_fusion = bf16[1024,2048]{1,0:T(8,128)(2,1)} fusion(bf16[512,1024]{1,0:T(8,128)(2,1)S(1)} %copy-done.12, bf16[512,2048]{1,0:T(8,128)(2,1)} %bitcast.68), kind=kOutput, calls=%fused_computation.1 | convolution fusion | flops 2149580800 | bytes 7340032 | tf_op jit(solution)/shard_map/dot_general | solution.py:1480
  353.5 69.8 %attention_backward.1 = (bf16[2,128,2048]{2,1,0:T(8,128)(2,1)}, bf16[2,128,2048]{2,1,0:T(8,128)(2,1)}, bf16[64,4096]{1,0:T(8,128)(2,1)}, bf16[4,64,256]{2,1,0:T(...) custom-call(bf16[512,2048]{1,0:T(8,128)(2,1)} %bitcast.69, ...), custom_call_target="tpu_custom_call" | custom-call | tf_op jit(solution)/shard_map/attention_backward/pallas_call | solution.py:1436
  424.2 1.4 collective-permute-start.1
  425.5 1.2 collective-permute-start.2
  426.7 1.8 collective-permute-start.3
  428.8 8.7 %convolution_bitcast_fusion.1 = f32[1,2048,768]{2,1,0:T(8,128)} fusion(bf16[1152,2048]{1,0:T(8,128)(2,1)} %get-tuple-element.103, bf16[1152,768]{1,0:T(8,128)(2,1)S(1)} %copy-done.6), kind=kOutput, calls=%fused_computation.3 | convolution fusion | flops 3623878656 | bytes 12779520 | tf_op jit(solution)/shard_map/dot_general | solution.py:1480
  437.6 6.3 %convolution_bitcast_fusion.2 = f32[1,2048,768]{2,1,0:T(8,128)} fusion(bf16[1152,2048]{1,0:T(8,128)(2,1)S(1)} %bitcast.81, bf16[1152,768]{1,0:T(8,128)(2,1)S(1)} %copy-done.5), kind=kOutput, calls=%fused_computation.4 | convolution fusion | flops 3623878656 | bytes 12779520 | tf_op jit(solution)/shard_map/dot_general | solution.py:1480
  445.1 0.9 fusion.8
  448.2 8.6 %convolution_bitcast_fusion = f32[1,768,2048]{2,1,0:T(8,128)} fusion(bf16[1152,768]{1,0:T(8,128)(2,1)S(1)} %copy-done.4, bf16[1152,2048]{1,0:T(8,128)(2,1)} %get-tuple-element.104), kind=kOutput, calls=%fused_computation.2 | convolution fusion | flops 3623878656 | bytes 12779520 | tf_op jit(solution)/shard_map/dot_general | solution.py:1480
  456.8 1.6 add_convert_fusion
  458.5 0.8 constant_dynamic-slice_fusion
  459.3 1.0 collective-permute-start.4
  462.2 2.1 convert_element_type.67
  464.3 1.3 dynamic_slice.6
  465.6 1.6 fusion.2
  467.2 3.1 collective-permute-done.4
  470.4 1.2 fusion.9
  471.5 6.8 %collective-permute-start.5 = (bf16[128,2048]{1,0:T(8,128)(2,1)S(1)}, bf16[128,2048]{1,0:T(8,128)(2,1)S(1)}, u32[]{:S(2)}, u32[]{:S(2)}) collective-permute-start(bf16[128,2048]{1,0:T(8,128)(2,1)S(1)} %fusion.9), channel_id=1, source_target_pairs={{0,0},{4,8},{8,16},{12,24},{16,4},{20,12},{24,20},{28,28},{1,1},{5... | collective-permute-start | bytes 1572872 | tf_op jit(solution)/shard_map/ppermute | solution.py:1564
  478.4 2.5 fusion.10
  480.8 9.8 %collective-permute-done.5 = bf16[128,2048]{1,0:T(8,128)(2,1)S(1)} collective-permute-done((bf16[128,2048]{1,0:T(8,128)(2,1)S(1)}, bf16[128,2048]{1,0:T(8,128)(2,1)S(1)}, u32[]{:S(2)}, u32[]{:S(2)}) %collective-permute-start.5) | collective-permute-done | bytes 524320 | tf_op jit(solution)/shard_map/ppermute | solution.py:1564
  490.6 1.1 convert_element_type.74
  (48 shorter events, 6.4 us)
Async XLA Ops:
  227.0 120.6 %copy-start.12 = (bf16[512,1024]{1,0:T(8,128)(2,1)S(1)}, bf16[512,1024]{1,0:T(8,128)(2,1)}, u32[]{:S(2)}) copy-start(bf16[512,1024]{1,0:T(8,128)(2,1)} %get-tuple-element.87) | copy-start | bytes 3145732
  353.5 75.0 %copy-start = (bf16[1,128,2048]{2,1,0:T(8,128)(2,1)S(1)}, bf16[1,128,2048]{2,1,0:T(8,128)(2,1)}, u32[]{:S(2)}) copy-start(bf16[1,128,2048]{2,1,0:T(8,128)(2,1)} %param.17) | copy-start | bytes 1572868
  353.5 75.2 %copy-start.6 = (bf16[1152,768]{1,0:T(8,128)(2,1)S(1)}, bf16[1152,768]{1,0:T(8,128)(2,1)}, u32[]{:S(2)}) copy-start(bf16[1152,768]{1,0:T(8,128)(2,1)} %get-tuple-element.71.dup) | copy-start | bytes 5308420
  353.5 84.0 %slice-start = ((s8[4718592]{0:T(1024)(128)(4,1)}), s8[524288]{0:T(1024)(128)(4,1)S(1)}, s32[]{:S(2)}) async-start(s8[4718592]{0:T(1024)(128)(4,1)} %bitcast.80), calls=%async_computation | async-start | bytes 1048576
  423.3 42.2 %collective-permute-start = (bf16[128,2048]{1,0:T(8,128)(2,1)}, bf16[128,2048]{1,0:T(8,128)(2,1)S(1)}, u32[]{:S(2)}, u32[]{:S(2)}) collective-permute-start(bf16[128,2048]{1,0:T(8,128)(2,1)} %get-tuple-element.93), channel_id=1, source_target_pairs={{0,4},{4,8},{8,12},{12,0},{1,5},{5,9},{9,13},{13,1},{2,6},{6,10},{... | collective-permute-start | bytes 1572872 | tf_op jit(solution)/shard_map/ppermute | solution.py:1551
  424.2 41.4 %collective-permute-start.1 = (bf16[128,2048]{1,0:T(8,128)(2,1)}, bf16[128,2048]{1,0:T(8,128)(2,1)S(1)}, u32[]{:S(2)}, u32[]{:S(2)}) collective-permute-start(bf16[128,2048]{1,0:T(8,128)(2,1)} %get-tuple-element.94), channel_id=1, source_target_pairs={{0,8},{4,12},{8,0},{12,4},{1,9},{5,13},{9,1},{13,5},{2,10},{6,14},... | collective-permute-start | bytes 1572872 | tf_op jit(solution)/shard_map/ppermute | solution.py:1551
  425.5 40.0 %collective-permute-start.2 = (bf16[128,2048]{1,0:T(8,128)(2,1)}, bf16[128,2048]{1,0:T(8,128)(2,1)}, u32[]{:S(2)}, u32[]{:S(2)}) collective-permute-start(bf16[128,2048]{1,0:T(8,128)(2,1)} %get-tuple-element.95), channel_id=1, source_target_pairs={{0,12},{4,0},{8,4},{12,8},{1,13},{5,1},{9,5},{13,9},{2,14},{6,2},{... | collective-permute-start | bytes 1572872 | tf_op jit(solution)/shard_map/ppermute | solution.py:1551
  426.7 30.1 %collective-permute-start.3 = (bf16[2,128,2048]{2,1,0:T(8,128)(2,1)}, bf16[2,128,2048]{2,1,0:T(8,128)(2,1)}, u32[]{:S(2)}, u32[]{:S(2)}) collective-permute-start(bf16[2,128,2048]{2,1,0:T(8,128)(2,1)} %get-tuple-element.101), channel_id=1, source_target_pairs={{0,2},{1,3},{2,0},{3,1},{4,6},{5,7},{6,4},{7,5},{8,10},{9,11},{10,... | collective-permute-start | bytes 3145736 | tf_op jit(solution)/shard_map/ppermute | solution.py:1554
  428.8 8.8 %copy-start.5 = (bf16[1152,768]{1,0:T(8,128)(2,1)S(1)}, bf16[1152,768]{1,0:T(8,128)(2,1)}, u32[]{:S(2)}) copy-start(bf16[1152,768]{1,0:T(8,128)(2,1)} %get-tuple-element.70.dgp) | copy-start | bytes 5308420
  428.8 8.8 %slice-start.1 = ((s8[4718592]{0:T(1024)(128)(4,1)}), s8[4194304]{0:T(1024)(128)(4,1)S(1)}, s32[]{:S(2)}) async-start(s8[4718592]{0:T(1024)(128)(4,1)} %bitcast.80), calls=%async_computation.1 | async-start | bytes 8388608
  437.5 6.3 %copy-start.3 = (bf16[4,128,2048]{2,1,0:T(8,128)(2,1)S(1)}, bf16[4,128,2048]{2,1,0:T(8,128)(2,1)}, u32[]{:S(2)}) copy-start(bf16[4,128,2048]{2,1,0:T(8,128)(2,1)} %get-tuple-element.90) | copy-start | bytes 6291460
  443.9 1.2 copy-start.1
  445.1 2.3 copy-start.9
  445.1 3.1 copy-start.10
  445.1 3.1 copy-start.4
  448.2 8.6 %copy-start.8 = (bf16[2,128,2048]{2,1,0:T(8,128)(2,1)S(1)}, bf16[2,128,2048]{2,1,0:T(8,128)(2,1)}, u32[]{:S(2)}) copy-start(bf16[2,128,2048]{2,1,0:T(8,128)(2,1)} %get-tuple-element.100) | copy-start | bytes 3145732
  458.4 7.1 %copy-start.2 = (bf16[128,2048]{1,0:T(8,128)(2,1)S(1)}, bf16[128,2048]{1,0:T(8,128)(2,1)}, u32[]{:S(2)}) copy-start(bf16[128,2048]{1,0:T(8,128)(2,1)} %get-tuple-element.92) | copy-start | bytes 1572868
  458.5 7.1 %copy-start.11 = (f32[1,2048]{1,0:T(1,128)S(1)}, f32[1,2048]{1,0:T(1,128)}, u32[]{:S(2)}) copy-start(f32[1,2048]{1,0:T(1,128)} %get-tuple-element.96) | copy-start | bytes 24580
  459.3 11.1 %collective-permute-start.4 = (bf16[1,128,2048]{2,1,0:T(8,128)(2,1)}, bf16[1,128,2048]{2,1,0:T(8,128)(2,1)}, u32[]{:S(2)}, u32[]{:S(2)}) collective-permute-start(bf16[1,128,2048]{2,1,0:T(8,128)(2,1)} %constant_dynamic-slice_fusion), channel_id=1, source_target_pairs={{0,1},{1,0},{2,3},{3,2},{4,5},{5,4},{6,7},{7,6},{8,9},{9,8},{10,11... | collective-permute-start | bytes 1572872 | tf_op jit(solution)/shard_map/ppermute | solution.py:1554
  465.6 12.8 %copy-start.7 = (f32[128,2048]{1,0:T(8,128)S(1)}, f32[128,2048]{1,0:T(8,128)}, u32[]{:S(2)}) copy-start(f32[128,2048]{1,0:T(8,128)} %get-tuple-element.91) | copy-start | bytes 3145732
  471.5 19.0 %collective-permute-start.5 = (bf16[128,2048]{1,0:T(8,128)(2,1)S(1)}, bf16[128,2048]{1,0:T(8,128)(2,1)S(1)}, u32[]{:S(2)}, u32[]{:S(2)}) collective-permute-start(bf16[128,2048]{1,0:T(8,128)(2,1)S(1)} %fusion.9), channel_id=1, source_target_pairs={{0,0},{4,8},{8,16},{12,24},{16,4},{20,12},{24,20},{28,28},{1,1},{5... | collective-permute-start | bytes 1572872 | tf_op jit(solution)/shard_map/ppermute | solution.py:1564

commit v2 on v1

--- a/solution.py
+++ b/solution.py
@@ -157,7 +157,7 @@
 def front_kernel(
     block, capacity, packed, experts,
     order, ids, slot_ids, tokens, wq, wk, wv, wo, router, norm_attn, norm_moe, cot, low_gains, frequency,
-    X_out, W_out, WO_out, PK, SM, G, out_out, q_out, k_out, v, mixed_out, xnt_out, gain_attn, gain_moe, gains,
+    X_out, W_out, WO_out, PK, SM, G, out_out, q_out, k_out, v, mixed_t, xnt_out, gain_attn, gain_moe, gains,
     cosine, sine, pos_col, pos_row, select_out, select_t_out, chosen, kept,
     X, W, WO, xn, kr, pack, out, q, mixed, xnt, select, select_t,
     local, save, zsend, zrecv, fsend, frecv, csend, crecv, wsend, wrecv,
@@ -343,7 +343,7 @@
         for i, (src, dst) in enumerate(
             (
                 (X, X_out), (W, W_out), (select, select_out), (select_t, select_t_out),
-                (WO, WO_out), (q, q_out), (mixed, mixed_out), (out, out_out), (xnt, xnt_out),
+                (WO, WO_out), (q, q_out), (out, out_out), (xnt, xnt_out),
             )
         )
     ]
@@ -408,7 +408,7 @@
                 c_copies[2][k + 1].start()
     for copy in c_copies[2]:
         copy.wait()
-    for copy in saves[4:7]:
+    for copy in saves[4:6]:
         copy.start()
 
     def project(j, carry):
@@ -419,7 +419,7 @@
         return carry
 
     lax.fori_loop(0, width // 256, project, 0)
-    saves[7].start()
+    saves[6].start()
 
     def turn(j, carry):
         cols = pl.ds(pl.multiple_of(j * 256, 256), 256)
@@ -427,7 +427,14 @@
         return carry
 
     lax.fori_loop(0, width // 256, turn, 0)
-    saves[8].start()
+    saves[7].start()
+
+    def turn_mixed(j, carry):
+        cols = pl.ds(pl.multiple_of(j * 256, 256), 256)
+        mixed_t[cols, :] = mixed[:, cols].T
+        return carry
+
+    lax.fori_loop(0, head_width // 256, turn_mixed, 0)
     g_line.hop(C - 1)
     x_line.finish()
     g_line.finish()
@@ -472,7 +479,7 @@
             sds((length, head_width), f32),
             sds((length, HEAD_DIM), f32),
             sds((length, HEAD_DIM), bf16),
-            sds((length, head_width), bf16),
+            sds((head_width, length), bf16),
             sds((width, length), bf16),
             sds((1, width), f32),
             sds((1, width), f32),
@@ -487,7 +494,7 @@
             sds((rows, wide), f32),
         ],
         in_specs=[pl.BlockSpec(memory_space=pltpu.SMEM), vm, vm] + [ANY] * 5 + [vm] * 3 + [ANY, vm, vm],
-        out_specs=[ANY] * 3 + [vm, vm] + [ANY] * 3 + [vm] * 2 + [ANY] * 2 + [vm] * 7 + [ANY] * 2 + [vm] * 2,
+        out_specs=[ANY] * 3 + [vm, vm] + [ANY] * 3 + [vm] * 3 + [ANY] + [vm] * 7 + [ANY] * 2 + [vm] * 2,
         scratch_shapes=[
             V((length, width), bf16),
             V(w_shape, bf16),
@@ -1150,13 +1157,13 @@
 
 
 def backward_kernel(
-    block, da, w_in, wo, q, k, v, xnt_in, x_in, cosine, sine, pos_col, pos_row, gains, go, sp, yp,
+    block, da, w_in, wo, q, k, v, xnt_in, x_in, cosine, sine, pos_col, pos_row, gains, mixed_t, sp, yp,
     OH, OX, Q3, KV3, S3, T3, YP, *rest,
 ):
     DX = rest[: lax.axis_size("ctx")]
     (
     w, xnt, x, late, dxn, dxsem, kr, dkr, dv, acc, DQ, head_grad,
-        GQ, Q1, Q2, QS, o_own, o_in, s_own, s_in, s_plane, s_sum, T, t_in, t_plane, t_sum,
+        GQ, Q1, Q2, QS, GO, o_in, s_own, s_in, s_plane, s_sum, T, t_in, t_plane, t_sum,
         local, qlocal, csend, crecv, fsend, frecv, zsend, zrecv, qcs, qcr, qfs, qfr, qzs, qzr, ysend, yrecv,
     ) = rest[lax.axis_size("ctx") :]
     S, C, F = sizes()
@@ -1175,9 +1182,9 @@
     sibling = (1 - s, c, f)
     cols = pl.ds(pl.multiple_of(step * wide, wide), wide)
 
-    o_first = remote(go.at[1 - s], o_in, csend.at[0], crecv.at[0], sibling)
+    o_own = GO.at[s]
+    o_first = remote(GO.at[1 - s], o_in, csend.at[0], crecv.at[0], sibling)
     t_first = remote(T, t_in, csend.at[2], crecv.at[2], sibling)
-    o_load = pltpu.make_async_copy(go.at[s], o_own, local.at[0])
     half = F // 2
     mine = lax.rem(f // half, 2)
     o_saves = [
@@ -1246,8 +1253,20 @@
         for copy in late_loads:
             copy.start()
         greet_all(z_peers + f_peers + [sibling])
-        for copy in [s_first, s_load, o_first, o_load] + y_copies:
+        for copy in [s_first, s_load] + y_copies:
             copy.start()
+
+        def out_rows(i, carry):
+            at, j = i // 4, lax.rem(i, 4)
+            part = mixed_t.shape[0] // S
+            rows = pl.ds(pl.multiple_of(at * part, 16), part)
+            lanes = pl.ds(pl.multiple_of(j * (width // 4), width // 4), width // 4)
+            piece = jnp.dot(mixed_t[rows, :], da[:, lanes], preferred_element_type=f32)
+            GO[at, :, :, lanes] = piece.astype(bf16).reshape(F, part // F, width // 4)
+            return carry
+
+        lax.fori_loop(0, S * 4, out_rows, 0)
+        o_first.start()
         unit, _ = rms_unit(k[...])
         kr[...] = half_turn(unit * gains[1:2, :], cosine[...], sine[...]).astype(bf16)
         dkr[...] = jnp.zeros_like(dkr)
@@ -1262,7 +1281,6 @@
     @pl.when(step == 1)
     def _():
         o_first.wait()
-        o_load.wait()
 
         def o_body(i, carry):
             o_own[i] = (o_own[i].astype(f32) + o_in[i].astype(f32)).astype(bf16)
@@ -1418,7 +1436,7 @@
                 copy.wait()
 
 
-def backward(da, w, wo, q, k, v, xnt, x, cosine, sine, pos_col, pos_row, gains, go, sp, yp):
+def backward(da, w, wo, q, k, v, xnt, x, cosine, sine, pos_col, pos_row, gains, mixed_t, sp, yp):
     S, C, F = sizes()
     length, width = x.shape
     head_width = wo.shape[0]
@@ -1431,7 +1449,7 @@
     whole = lambda array: pl.BlockSpec(array.shape, lambda i: (0, 0), pipeline_mode=once)
     sds = jax.ShapeDtypeStruct
     V = pltpu.VMEM
-    q_block, o_block, s_block = (shard, wide), go.shape[2:], sp.shape[3:]
+    q_block, o_block, s_block = (shard, wide), (head_width // (S * F), width), sp.shape[3:]
     t_block = (width // HEAD_DIM + 8, HEAD_DIM)
     return pl.pallas_call(
         functools.partial(backward_kernel, block),
@@ -1449,8 +1467,8 @@
         in_specs=[whole(da), ANY, whole(wo)]
         + [pl.BlockSpec((length, wide), lambda i: (0, jnp.minimum(i, pairs - 1)))]
         + [whole(k), whole(v), ANY, ANY]
-        + [whole(array) for array in (cosine, sine, pos_col, pos_row, gains)]
-        + [ANY] * 3,
+        + [whole(array) for array in (cosine, sine, pos_col, pos_row, gains, mixed_t)]
+        + [ANY] * 2,
         out_specs=[ANY] * (7 + C),
         scratch_shapes=[
             V(w.shape, bf16), V(xnt.shape, bf16), V(x.shape, bf16), DMA((3,)),
@@ -1459,7 +1477,7 @@
             V((length, width), f32), V((length, wide), bf16), V((8, HEAD_DIM), f32),
             V((units, S, C, F) + q_block, bf16), V((units, C, F) + q_block, bf16),
             V((units, F - 1, C) + q_block, bf16), V((units, C) + q_block, bf16),
-            V((F,) + o_block, bf16), V((F,) + o_block, bf16),
+            V((S, F) + o_block, bf16), V((F,) + o_block, bf16),
             V((C, F) + s_block, bf16), V((C, F) + s_block, bf16), V((F - 1, C) + s_block, bf16), V((C,) + s_block, bf16),
             V(t_block, f32), V(t_block, f32), V((F - 1,) + t_block, f32), V(t_block, f32),
             DMA((7,)), DMA((units,)),
@@ -1469,7 +1487,7 @@
         ],
         name="attention_backward",
         compiler_params=params(7, 60 * 2**20),
-    )(da, w, wo, q, k, v, xnt, x, cosine, sine, pos_col, pos_row, gains, go, sp, yp)
+    )(da, w, wo, q, k, v, xnt, x, cosine, sine, pos_col, pos_row, gains, mixed_t, sp, yp)
 
 
 def dot(left, right):
@@ -1515,7 +1533,7 @@
     shard = w_router.shape[0]
     pack_width = round_up(experts + 2, 128)
     (
-        X, W, WO, PK, _, G, out_part, q, k, v, mixed, xnt, gain_attn, gain_moe, gains,
+        X, W, WO, PK, _, G, out_part, q, k, v, mixed_t, xnt, gain_attn, gain_moe, gains,
         cosine, sine, pos_col, pos_row, select, select_t, chosen, kept_map,
     ) = front(
         capacity, packed, stretch_order, expert_ids[0].T, slot_index[0].T,
@@ -1534,15 +1552,13 @@
         xm, hidden, dgp, dup, w_gate, w_up, w_down,
     )
     DA = DA.reshape(length, width)
-    grad_out_part = contract_rows(mixed, DA).astype(bf16)
-    out_parts = grad_out_part.reshape(S, F, head_width // Q, width)
 
     def part_of(parts, at):
         return lax.dynamic_index_in_dim(parts, at, 0, keepdims=False)
 
     out_half, out_other, query_sum, kv_sums, small_sums, tiny_sums, y_parts, *dxn_parts = backward(
         DA, W, WO, q, k, v, xnt, X, cosine, sine, pos_col, pos_row, gains,
-        out_parts,
+        mixed_t,
         small.reshape(S, C, F, shard, pack_width),
         y_part.reshape(C, rows, width),
     )

time: 495 us -> 491 us (level)
    dot_general x4 -> x3, matrix products: 29.6 us -> 25.9 us  [contract_rows(): lax.dot_general(left, right, (((0,), (0,)), ((), ())), preferred_element_...]
where the time goes in v2:
time: 491 us; the launch traced here: 487 us
  Pallas kernels  417 us (85%)
  matrix products  25.9 us (5%)
  other arithmetic  12.3 us (3%)
  starting transfers between devices  12.2 us (2%)
  waiting for transfers between devices  12.2 us (2%)
  local copies, waits for them, and re-layouts  6.25 us (1%)
    pallas_call x1, Pallas kernels, dispatch(): pl.pallas_call(functools.partial(dispatch_kernel, packed), out_shape=[sds...  121 us
    pallas_call x1, Pallas kernels, give_back(): pl.pallas_call(functools.partial(return_kernel, packed, experts), out_sha...  120 us
    pallas_call x1, Pallas kernels, front(): pl.pallas_call(functools.partial(front_kernel, block, capacity, packed, e...  106 us
    pallas_call x1, Pallas kernels, backward(): pl.pallas_call(functools.partial(backward_kernel, block), out_shape=[sds(...  70.5 us
    dot_general x3, matrix products, contract_rows(): lax.dot_general(left, right, (((0,), (0,)), ((), ())), preferred_element_...  25.9 us
  transfers between devices with their start and end apart: 6, of which 2 were waited for; matrix products, arithmetic and copies ran while one was open for 8% of the time, Pallas kernels for 0%

profile of v2, /device:TPU:1, one launch (start us, length us, event | category | flops | bytes accessed | tf_op | source)
XLA Modules:
  0.0 487.3 jit_solution(9841993991332983160)
XLA Ops:
  0.6 105.5 %gather_and_attend.1 = (bf16[512,2048]{1,0:T(8,128)(2,1)}, bf16[2,4,4,64,1280]{4,3,2,1,0:T(8,128)(2,1)}, bf16[2,4,128,2048]{3,2,1,0:T(8,128)(2,1)}, bf16[2,4,4,6...) custom-call(s32[8]{0:T(128)} %order.1, ...), custom_call_target="tpu_custom_call" | custom-call | tf_op jit(solution)/shard_map/gather_and_attend/pallas_call | solution.py:469
  106.2 121.1 %dispatch_rows.1 = (bf16[1152,2048]{1,0:T(8,128)(2,1)}, bf16[1152,2048]{1,0:T(8,128)(2,1)}, f32[8,8,256]{2,1,0:T(8,128)}, f32[128,2048]{1,0:T(8,128)}, bf16[128,...) custom-call(bf16[4,128,2048]{2,1,0:T(8,128)(2,1)} %bitcast.61, ...), custom_call_target="tpu_custom_call" | custom-call | tf_op jit(solution)/shard_map/dispatch_rows/pallas_call | solution.py:856
  227.3 120.2 %return_grads.1 = (bf16[4,128,2048]{2,1,0:T(8,128)(2,1)}, bf16[512,2048]{1,0:T(8,128)(2,1)}, f32[128,2048]{1,0:T(8,128)}, bf16[2048,128]{1,0:T(8,128)(2,1)}) custom-call(f32[8,8,256]{2,1,0:T(8,128)} %get-tuple-element.67.dgr, f32[128,128]{1,0:T(8,128)} %get-tuple-element.68.gates, bf16[2048,128]{1,0:T(8,128)(2,1)} %bitcast.63, ...), custom_call_target="tpu_custom_call" | custom-call | tf_op jit(solution)/shard_map/return_grads/pallas_call | solution.py:1119
  347.6 70.5 %attention_backward.1 = (bf16[2,128,2048]{2,1,0:T(8,128)(2,1)}, bf16[2,128,2048]{2,1,0:T(8,128)(2,1)}, bf16[64,4096]{1,0:T(8,128)(2,1)}, bf16[4,64,256]{2,1,0:T(...) custom-call(bf16[512,2048]{1,0:T(8,128)(2,1)} %bitcast.58, ...), custom_call_target="tpu_custom_call" | custom-call | tf_op jit(solution)/shard_map/attention_backward/pallas_call | solution.py:1454
  418.1 0.9 collective-permute-start
  418.9 1.3 collective-permute-start.1
  420.2 1.2 collective-permute-start.2
  421.4 1.8 collective-permute-start.3
  423.3 8.7 %convolution_bitcast_fusion.1 = f32[1,2048,768]{2,1,0:T(8,128)} fusion(bf16[1152,2048]{1,0:T(8,128)(2,1)} %get-tuple-element.103, bf16[1152,768]{1,0:T(8,128)(2,1)S(1)} %copy-done.6), kind=kOutput, calls=%fused_computation.2 | convolution fusion | flops 3623878656 | bytes 12779520 | tf_op jit(solution)/shard_map/dot_general | solution.py:1498
  432.0 8.6 %convolution_bitcast_fusion.2 = f32[1,2048,768]{2,1,0:T(8,128)} fusion(bf16[1152,2048]{1,0:T(8,128)(2,1)} %get-tuple-element.103, bf16[1152,768]{1,0:T(8,128)(2,1)S(1)} %copy-done.5), kind=kOutput, calls=%fused_computation.3 | convolution fusion | flops 3623878656 | bytes 12779520 | tf_op jit(solution)/shard_map/dot_general | solution.py:1498
  441.8 0.9 fusion.8
  444.9 8.6 %convolution_bitcast_fusion = f32[1,768,2048]{2,1,0:T(8,128)} fusion(bf16[1152,768]{1,0:T(8,128)(2,1)S(1)} %copy-done.4, bf16[1152,2048]{1,0:T(8,128)(2,1)} %get-tuple-element.104), kind=kOutput, calls=%fused_computation.1 | convolution fusion | flops 3623878656 | bytes 12779520 | tf_op jit(solution)/shard_map/dot_general | solution.py:1498
  453.6 1.6 add_convert_fusion
  455.2 0.8 constant_dynamic-slice_fusion
  456.0 1.6 collective-permute-start.4
  459.6 2.1 convert_element_type.63
  461.6 1.3 dynamic_slice.6
  463.0 1.6 fusion.2
  464.6 2.8 collective-permute-done.4
  467.4 1.2 fusion.9
  468.5 5.5 %collective-permute-start.5 = (bf16[128,2048]{1,0:T(8,128)(2,1)S(1)}, bf16[128,2048]{1,0:T(8,128)(2,1)S(1)}, u32[]{:S(2)}, u32[]{:S(2)}) collective-permute-start(bf16[128,2048]{1,0:T(8,128)(2,1)S(1)} %fusion.9), channel_id=1, source_target_pairs={{0,0},{4,8},{8,16},{12,24},{16,4},{20,12},{24,20},{28,28},{1,1},{5... | collective-permute-start | bytes 1572872 | tf_op jit(solution)/shard_map/ppermute | solution.py:1580
  474.1 2.5 fusion.10
  476.5 9.5 %collective-permute-done.5 = bf16[128,2048]{1,0:T(8,128)(2,1)S(1)} collective-permute-done((bf16[128,2048]{1,0:T(8,128)(2,1)S(1)}, bf16[128,2048]{1,0:T(8,128)(2,1)S(1)}, u32[]{:S(2)}, u32[]{:S(2)}) %collective-permute-start.5) | collective-permute-done | bytes 524320 | tf_op jit(solution)/shard_map/ppermute | solution.py:1580
  486.0 1.1 convert_element_type.70
  (40 shorter events, 5.6 us)
Async XLA Ops:
  347.6 75.6 %copy-start = (bf16[1,128,2048]{2,1,0:T(8,128)(2,1)S(1)}, bf16[1,128,2048]{2,1,0:T(8,128)(2,1)}, u32[]{:S(2)}) copy-start(bf16[1,128,2048]{2,1,0:T(8,128)(2,1)} %param.17) | copy-start | bytes 1572868
  347.6 75.8 %copy-start.6 = (bf16[1152,768]{1,0:T(8,128)(2,1)S(1)}, bf16[1152,768]{1,0:T(8,128)(2,1)}, u32[]{:S(2)}) copy-start(bf16[1152,768]{1,0:T(8,128)(2,1)} %get-tuple-element.71.dup) | copy-start | bytes 5308420
  418.1 44.9 %collective-permute-start = (bf16[128,2048]{1,0:T(8,128)(2,1)}, bf16[128,2048]{1,0:T(8,128)(2,1)S(1)}, u32[]{:S(2)}, u32[]{:S(2)}) collective-permute-start(bf16[128,2048]{1,0:T(8,128)(2,1)} %get-tuple-element.93), channel_id=1, source_target_pairs={{0,4},{4,8},{8,12},{12,0},{1,5},{5,9},{9,13},{13,1},{2,6},{6,10},{... | collective-permute-start | bytes 1572872 | tf_op jit(solution)/shard_map/ppermute | solution.py:1567
  418.9 44.0 %collective-permute-start.1 = (bf16[128,2048]{1,0:T(8,128)(2,1)}, bf16[128,2048]{1,0:T(8,128)(2,1)S(1)}, u32[]{:S(2)}, u32[]{:S(2)}) collective-permute-start(bf16[128,2048]{1,0:T(8,128)(2,1)} %get-tuple-element.94), channel_id=1, source_target_pairs={{0,8},{4,12},{8,0},{12,4},{1,9},{5,13},{9,1},{13,5},{2,10},{6,14},... | collective-permute-start | bytes 1572872 | tf_op jit(solution)/shard_map/ppermute | solution.py:1567
  420.2 42.7 %collective-permute-start.2 = (bf16[128,2048]{1,0:T(8,128)(2,1)}, bf16[128,2048]{1,0:T(8,128)(2,1)}, u32[]{:S(2)}, u32[]{:S(2)}) collective-permute-start(bf16[128,2048]{1,0:T(8,128)(2,1)} %get-tuple-element.95), channel_id=1, source_target_pairs={{0,12},{4,0},{8,4},{12,8},{1,13},{5,1},{9,5},{13,9},{2,14},{6,2},{... | collective-permute-start | bytes 1572872 | tf_op jit(solution)/shard_map/ppermute | solution.py:1567
  421.4 32.2 %collective-permute-start.3 = (bf16[2,128,2048]{2,1,0:T(8,128)(2,1)}, bf16[2,128,2048]{2,1,0:T(8,128)(2,1)}, u32[]{:S(2)}, u32[]{:S(2)}) collective-permute-start(bf16[2,128,2048]{2,1,0:T(8,128)(2,1)} %get-tuple-element.101), channel_id=1, source_target_pairs={{0,2},{1,3},{2,0},{3,1},{4,6},{5,7},{6,4},{7,5},{8,10},{9,11},{10,... | collective-permute-start | bytes 3145736 | tf_op jit(solution)/shard_map/ppermute | solution.py:1570
  423.3 8.7 %copy-start.5 = (bf16[1152,768]{1,0:T(8,128)(2,1)S(1)}, bf16[1152,768]{1,0:T(8,128)(2,1)}, u32[]{:S(2)}) copy-start(bf16[1152,768]{1,0:T(8,128)(2,1)} %get-tuple-element.70.dgp) | copy-start | bytes 5308420
  432.0 8.6 %copy-start.3 = (bf16[4,128,2048]{2,1,0:T(8,128)(2,1)S(1)}, bf16[4,128,2048]{2,1,0:T(8,128)(2,1)}, u32[]{:S(2)}) copy-start(bf16[4,128,2048]{2,1,0:T(8,128)(2,1)} %get-tuple-element.90) | copy-start | bytes 6291460
  440.6 1.2 copy-start.1
  441.8 2.3 copy-start.9
  441.8 3.1 copy-start.10
  441.8 3.1 copy-start.4
  444.9 8.6 %copy-start.8 = (bf16[2,128,2048]{2,1,0:T(8,128)(2,1)S(1)}, bf16[2,128,2048]{2,1,0:T(8,128)(2,1)}, u32[]{:S(2)}) copy-start(bf16[2,128,2048]{2,1,0:T(8,128)(2,1)} %get-tuple-element.100) | copy-start | bytes 3145732
  455.2 7.8 %copy-start.2 = (bf16[128,2048]{1,0:T(8,128)(2,1)S(1)}, bf16[128,2048]{1,0:T(8,128)(2,1)}, u32[]{:S(2)}) copy-start(bf16[128,2048]{1,0:T(8,128)(2,1)} %get-tuple-element.92) | copy-start | bytes 1572868
  455.2 7.8 %copy-start.11 = (f32[1,2048]{1,0:T(1,128)S(1)}, f32[1,2048]{1,0:T(1,128)}, u32[]{:S(2)}) copy-start(f32[1,2048]{1,0:T(1,128)} %get-tuple-element.96) | copy-start | bytes 24580
  456.0 11.3 %collective-permute-start.4 = (bf16[1,128,2048]{2,1,0:T(8,128)(2,1)}, bf16[1,128,2048]{2,1,0:T(8,128)(2,1)}, u32[]{:S(2)}, u32[]{:S(2)}) collective-permute-start(bf16[1,128,2048]{2,1,0:T(8,128)(2,1)} %constant_dynamic-slice_fusion), channel_id=1, source_target_pairs={{0,1},{1,0},{2,3},{3,2},{4,5},{5,4},{6,7},{7,6},{8,9},{9,8},{10,11... | collective-permute-start | bytes 1572872 | tf_op jit(solution)/shard_map/ppermute | solution.py:1570
  462.9 11.1 %copy-start.7 = (f32[128,2048]{1,0:T(8,128)S(1)}, f32[128,2048]{1,0:T(8,128)}, u32[]{:S(2)}) copy-start(f32[128,2048]{1,0:T(8,128)} %get-tuple-element.91) | copy-start | bytes 3145732
  468.5 17.5 %collective-permute-start.5 = (bf16[128,2048]{1,0:T(8,128)(2,1)S(1)}, bf16[128,2048]{1,0:T(8,128)(2,1)S(1)}, u32[]{:S(2)}, u32[]{:S(2)}) collective-permute-start(bf16[128,2048]{1,0:T(8,128)(2,1)S(1)} %fusion.9), channel_id=1, source_target_pairs={{0,0},{4,8},{8,16},{12,24},{16,4},{20,12},{24,20},{28,28},{1,1},{5... | collective-permute-start | bytes 1572872 | tf_op jit(solution)/shard_map/ppermute | solution.py:1580

commit v3 on v2

--- a/solution.py
+++ b/solution.py
@@ -1572,6 +1572,7 @@
         bit //= 2
         if not bit:
             break
+        out_sum, hidden, slot_grad = lax.optimization_barrier((out_sum, hidden, slot_grad))
         mine = lax.rem(fsdp_at // bit, 2)
         parts = out_sum.reshape((2, bit) + out_sum.shape[1:])
         out_sum, out_other = part_of(parts, mine), part_of(parts, 1 - mine)

time: 491 us -> 505 us (1.029)
  starting transfers between devices: 12.2 us -> 21.8 us
  waiting for transfers between devices: 12.2 us -> 21.3 us
    ppermute x3, waiting for transfers between devices: 0.01 us -> 10.5 us  [on_device(): lax.ppermute(dxn_parts[i], 'ctx', [(j, (j + i) % C) for j in range(C)])]
    ppermute x1, starting transfers between devices: 5.55 us -> 15 us  [on_device(): o_sum = lax.ppermute(out_sum, ('seq', 'ctx'), turn)]
    ppermute x1, waiting for transfers between devices: 9.47 us -> 2.42 us  [on_device(): o_sum = lax.ppermute(out_sum, ('seq', 'ctx'), turn)]
    ppermute x2, waiting for transfers between devices: 2.77 us -> 8.3 us  [on_device(): came = lax.ppermute(out_other, 'fsdp', [(i, i ^ bit) for i in range(F)])]
  transfers between devices with their start and end apart: 6 -> 6, of which waited for: 2 -> 3; matrix products, arithmetic and copies ran while one was open for 8% -> 7% of each run, Pallas kernels for 0% -> 0%
where the time goes in v3:
time: 505 us; the launch traced here: 502 us
  Pallas kernels  417 us (83%)
  matrix products  25.8 us (5%)
  starting transfers between devices  21.8 us (4%)
  waiting for transfers between devices  21.3 us (4%)
  other arithmetic  11.3 us (2%)
    pallas_call x1, Pallas kernels, dispatch(): pl.pallas_call(functools.partial(dispatch_kernel, packed), out_shape=[sds...  121 us
    pallas_call x1, Pallas kernels, give_back(): pl.pallas_call(functools.partial(return_kernel, packed, experts), out_sha...  120 us
    pallas_call x1, Pallas kernels, front(): pl.pallas_call(functools.partial(front_kernel, block, capacity, packed, e...  106 us
    pallas_call x1, Pallas kernels, backward(): pl.pallas_call(functools.partial(backward_kernel, block), out_shape=[sds(...  70.3 us
    dot_general x3, matrix products, contract_rows(): lax.dot_general(left, right, (((0,), (0,)), ((), ())), preferred_element_...  25.8 us
    ppermute x1, starting transfers between devices, on_device(): o_sum = lax.ppermute(out_sum, ('seq', 'ctx'), turn)  15 us
    ppermute x3, waiting for transfers between devices, on_device(): lax.ppermute(dxn_parts[i], 'ctx', [(j, (j + i) % C) for j in range(C)])  10.5 us
  transfers between devices with their start and end apart: 6, of which 3 were waited for; matrix products, arithmetic and copies ran while one was open for 7% of the time, Pallas kernels for 0%

profile of v3, /device:TPU:1, one launch (start us, length us, event | category | flops | bytes accessed | tf_op | source)
XLA Modules:
  0.0 502.0 jit_solution(4197991737528567426)
XLA Ops:
  0.6 105.6 %gather_and_attend.1 = (bf16[512,2048]{1,0:T(8,128)(2,1)}, bf16[2,4,4,64,1280]{4,3,2,1,0:T(8,128)(2,1)}, bf16[2,4,128,2048]{3,2,1,0:T(8,128)(2,1)}, bf16[2,4,4,6...) custom-call(s32[8]{0:T(128)} %order.1, ...), custom_call_target="tpu_custom_call" | custom-call | tf_op jit(solution)/shard_map/gather_and_attend/pallas_call | solution.py:469
  106.2 121.1 %dispatch_rows.1 = (bf16[1152,2048]{1,0:T(8,128)(2,1)}, bf16[1152,2048]{1,0:T(8,128)(2,1)}, f32[8,8,256]{2,1,0:T(8,128)}, f32[128,2048]{1,0:T(8,128)}, bf16[128,...) custom-call(bf16[4,128,2048]{2,1,0:T(8,128)(2,1)} %bitcast.61, ...), custom_call_target="tpu_custom_call" | custom-call | tf_op jit(solution)/shard_map/dispatch_rows/pallas_call | solution.py:856
  227.4 120.3 %return_grads.1 = (bf16[4,128,2048]{2,1,0:T(8,128)(2,1)}, bf16[512,2048]{1,0:T(8,128)(2,1)}, f32[128,2048]{1,0:T(8,128)}, bf16[2048,128]{1,0:T(8,128)(2,1)}) custom-call(f32[8,8,256]{2,1,0:T(8,128)} %get-tuple-element.70.dgr, f32[128,128]{1,0:T(8,128)} %get-tuple-element.71.gates, bf16[2048,128]{1,0:T(8,128)(2,1)} %bitcast.63, ...), custom_call_target="tpu_custom_call" | custom-call | tf_op jit(solution)/shard_map/return_grads/pallas_call | solution.py:1119
  347.7 70.3 %attention_backward.1 = (bf16[2,128,2048]{2,1,0:T(8,128)(2,1)}, bf16[2,128,2048]{2,1,0:T(8,128)(2,1)}, bf16[64,4096]{1,0:T(8,128)(2,1)}, bf16[4,64,256]{2,1,0:T(...) custom-call(bf16[512,2048]{1,0:T(8,128)(2,1)} %bitcast.58, ...), custom_call_target="tpu_custom_call" | custom-call | tf_op jit(solution)/shard_map/attention_backward/pallas_call | solution.py:1454
  418.0 2.0 collective-permute-start.3
  420.0 0.8 collective-permute-start
  420.8 1.0 collective-permute-start.1
  421.8 1.5 collective-permute-start.2
  423.3 8.7 %convolution_bitcast_fusion.1 = f32[1,2048,768]{2,1,0:T(8,128)} fusion(bf16[1152,2048]{1,0:T(8,128)(2,1)} %get-tuple-element.108, bf16[1152,768]{1,0:T(8,128)(2,1)S(1)} %copy-done.6), kind=kOutput, calls=%fused_computation.2 | convolution fusion | flops 3623878656 | bytes 12779520 | tf_op jit(solution)/shard_map/dot_general | solution.py:1498
  432.0 8.6 %convolution_bitcast_fusion.2 = f32[1,2048,768]{2,1,0:T(8,128)} fusion(bf16[1152,2048]{1,0:T(8,128)(2,1)} %get-tuple-element.108, bf16[1152,768]{1,0:T(8,128)(2,1)S(1)} %copy-done.5), kind=kOutput, calls=%fused_computation.3 | convolution fusion | flops 3623878656 | bytes 12779520 | tf_op jit(solution)/shard_map/dot_general | solution.py:1498
  441.4 0.7 copy_bitcast_fusion
  442.2 0.7 slice_reduce_fusion
  443.4 2.1 convert_element_type.63
  446.8 0.9 fusion.8
  447.7 10.5 %collective-permute-done.1 = bf16[128,2048]{1,0:T(8,128)(2,1)} collective-permute-done((bf16[128,2048]{1,0:T(8,128)(2,1)}, bf16[128,2048]{1,0:T(8,128)(2,1)}, u32[]{:S(2)}, u32[]{:S(2)}) %collective-permute-start.1) | collective-permute-done | bytes 524320 | tf_op jit(solution)/shard_map/ppermute | solution.py:1567
  458.3 1.9 fusion.2
  460.2 1.7 add_convert_fusion
  461.9 1.5 collective-permute-start.4
  463.5 2.9 fusion.10
  466.4 8.3 %collective-permute-done.4 = bf16[1,128,2048]{2,1,0:T(8,128)(2,1)S(1)} collective-permute-done((bf16[1,128,2048]{2,1,0:T(8,128)(2,1)S(1)}, bf16[1,128,2048]{2,1,0:T(8,128)(2,1)S(1)}, u32[]{:S(2)}, u32[]{:S(2)}) %collective-permute-start.4) | collective-permute-done | bytes 524320 | tf_op jit(solution)/shard_map/ppermute | solution.py:1570
  474.8 15.0 %collective-permute-start.5 = (bf16[128,2048]{1,0:T(8,128)(2,1)S(1)}, bf16[128,2048]{1,0:T(8,128)(2,1)S(1)}, u32[]{:S(2)}, u32[]{:S(2)}) collective-permute-start(bf16[128,2048]{1,0:T(8,128)(2,1)S(1)} %fusion.9), channel_id=1, source_target_pairs={{0,0},{4,8},{8,16},{12,24},{16,4},{20,12},{24,20},{28,28},{1,1},{5... | collective-permute-start | bytes 1572872 | tf_op jit(solution)/shard_map/ppermute | solution.py:1581
  489.8 8.5 %convolution_bitcast_fusion = f32[1,768,2048]{2,1,0:T(8,128)} fusion(bf16[1152,768]{1,0:T(8,128)(2,1)S(1)} %copy-done.4, bf16[1152,2048]{1,0:T(8,128)(2,1)} %get-tuple-element.110), kind=kOutput, calls=%fused_computation.1 | convolution fusion | flops 3623878656 | bytes 12779520 | tf_op jit(solution)/shard_map/dot_general | solution.py:1498
  498.3 2.4 collective-permute-done.5
  500.8 1.1 convert_element_type.70
  (42 shorter events, 2.9 us)
Async XLA Ops:
  347.7 75.6 %copy-start.6 = (bf16[1152,768]{1,0:T(8,128)(2,1)S(1)}, bf16[1152,768]{1,0:T(8,128)(2,1)}, u32[]{:S(2)}) copy-start(bf16[1152,768]{1,0:T(8,128)(2,1)} %get-tuple-element.74.dup) | copy-start | bytes 5308420
  418.0 42.1 %collective-permute-start.3 = (bf16[2,128,2048]{2,1,0:T(8,128)(2,1)}, bf16[2,128,2048]{2,1,0:T(8,128)(2,1)}, u32[]{:S(2)}, u32[]{:S(2)}) collective-permute-start(bf16[2,128,2048]{2,1,0:T(8,128)(2,1)} %get-tuple-element.104), channel_id=1, source_target_pairs={{0,2},{1,3},{2,0},{3,1},{4,6},{5,7},{6,4},{7,5},{8,10},{9,11},{10,... | collective-permute-start | bytes 3145736 | tf_op jit(solution)/shard_map/ppermute | solution.py:1570
  420.0 27.7 %collective-permute-start = (bf16[128,2048]{1,0:T(8,128)(2,1)}, bf16[128,2048]{1,0:T(8,128)(2,1)}, u32[]{:S(2)}, u32[]{:S(2)}) collective-permute-start(bf16[128,2048]{1,0:T(8,128)(2,1)} %get-tuple-element.96), channel_id=1, source_target_pairs={{0,4},{4,8},{8,12},{12,0},{1,5},{5,9},{9,13},{13,1},{2,6},{6,10},{... | collective-permute-start | bytes 1572872 | tf_op jit(solution)/shard_map/ppermute | solution.py:1567
  420.8 37.5 %collective-permute-start.1 = (bf16[128,2048]{1,0:T(8,128)(2,1)}, bf16[128,2048]{1,0:T(8,128)(2,1)}, u32[]{:S(2)}, u32[]{:S(2)}) collective-permute-start(bf16[128,2048]{1,0:T(8,128)(2,1)} %get-tuple-element.97), channel_id=1, source_target_pairs={{0,8},{4,12},{8,0},{12,4},{1,9},{5,13},{9,1},{13,5},{2,10},{6,14},... | collective-permute-start | bytes 1572872 | tf_op jit(solution)/shard_map/ppermute | solution.py:1567
  421.8 36.5 %collective-permute-start.2 = (bf16[128,2048]{1,0:T(8,128)(2,1)}, bf16[128,2048]{1,0:T(8,128)(2,1)}, u32[]{:S(2)}, u32[]{:S(2)}) collective-permute-start(bf16[128,2048]{1,0:T(8,128)(2,1)} %get-tuple-element.98), channel_id=1, source_target_pairs={{0,12},{4,0},{8,4},{12,8},{1,13},{5,1},{9,5},{13,9},{2,14},{6,2},{... | collective-permute-start | bytes 1572872 | tf_op jit(solution)/shard_map/ppermute | solution.py:1567
  423.3 8.7 %copy-start.5 = (bf16[1152,768]{1,0:T(8,128)(2,1)S(1)}, bf16[1152,768]{1,0:T(8,128)(2,1)}, u32[]{:S(2)}) copy-start(bf16[1152,768]{1,0:T(8,128)(2,1)} %get-tuple-element.73.dgp) | copy-start | bytes 5308420
  432.0 8.6 %copy-start = (bf16[1,128,2048]{2,1,0:T(8,128)(2,1)S(1)}, bf16[1,128,2048]{2,1,0:T(8,128)(2,1)}, u32[]{:S(2)}) copy-start(bf16[1,128,2048]{2,1,0:T(8,128)(2,1)} %param.17) | copy-start | bytes 1572868
  432.0 8.8 %copy-start.9 = (bf16[4,64,256]{2,1,0:T(8,128)(2,1)S(1)}, bf16[4,64,256]{2,1,0:T(8,128)(2,1)}, u32[]{:S(2)}) copy-start(bf16[4,64,256]{2,1,0:T(8,128)(2,1)} %get-tuple-element.102) | copy-start | bytes 393220
  432.0 8.8 %copy-start.3 = (bf16[4,128,2048]{2,1,0:T(8,128)(2,1)S(1)}, bf16[4,128,2048]{2,1,0:T(8,128)(2,1)}, u32[]{:S(2)}) copy-start(bf16[4,128,2048]{2,1,0:T(8,128)(2,1)} %get-tuple-element.93) | copy-start | bytes 6291460
  440.5 0.8 copy-start.10
  440.6 0.9 copy-start.11
  440.8 6.0 %copy-start.1 = (f32[128,2048]{1,0:T(8,128)S(1)}, f32[128,2048]{1,0:T(8,128)}, u32[]{:S(2)}) copy-start(f32[128,2048]{1,0:T(8,128)} %get-tuple-element.69.h1) | copy-start | bytes 3145732
  443.4 14.9 %copy-start.2 = (bf16[128,2048]{1,0:T(8,128)(2,1)S(1)}, bf16[128,2048]{1,0:T(8,128)(2,1)}, u32[]{:S(2)}) copy-start(bf16[128,2048]{1,0:T(8,128)(2,1)} %get-tuple-element.95) | copy-start | bytes 1572868
  443.4 14.9 %copy-start.12 = (f32[1,2048]{1,0:T(1,128)S(1)}, f32[1,2048]{1,0:T(1,128)}, u32[]{:S(2)}) copy-start(f32[1,2048]{1,0:T(1,128)} %get-tuple-element.99) | copy-start | bytes 24580
  446.8 13.3 %copy-start.8 = (bf16[2,128,2048]{2,1,0:T(8,128)(2,1)S(1)}, bf16[2,128,2048]{2,1,0:T(8,128)(2,1)}, u32[]{:S(2)}) copy-start(bf16[2,128,2048]{2,1,0:T(8,128)(2,1)} %get-tuple-element.103) | copy-start | bytes 3145732
  460.2 3.3 copy-start.7
  461.9 12.7 %collective-permute-start.4 = (bf16[1,128,2048]{2,1,0:T(8,128)(2,1)S(1)}, bf16[1,128,2048]{2,1,0:T(8,128)(2,1)S(1)}, u32[]{:S(2)}, u32[]{:S(2)}) collective-permute-start(bf16[1,128,2048]{2,1,0:T(8,128)(2,1)S(1)} %constant_dynamic-slice_fusion), channel_id=1, source_target_pairs={{0,1},{1,0},{2,3},{3,2},{4,5},{5,4},{6,7},{7,6},{8,9},{9,8},{10,11... | collective-permute-start | bytes 1572872 | tf_op jit(solution)/shard_map/ppermute | solution.py:1570
  463.5 26.3 %copy-start.4 = (bf16[1152,768]{1,0:T(8,128)(2,1)S(1)}, bf16[1152,768]{1,0:T(8,128)(2,1)}, u32[]{:S(2)}) copy-start(bf16[1152,768]{1,0:T(8,128)(2,1)} %get-tuple-element.109.hidden_in) | copy-start | bytes 5308420
  474.8 26.0 %collective-permute-start.5 = (bf16[128,2048]{1,0:T(8,128)(2,1)S(1)}, bf16[128,2048]{1,0:T(8,128)(2,1)S(1)}, u32[]{:S(2)}, u32[]{:S(2)}) collective-permute-start(bf16[128,2048]{1,0:T(8,128)(2,1)S(1)} %fusion.9), channel_id=1, source_target_pairs={{0,0},{4,8},{8,16},{12,24},{16,4},{20,12},{24,20},{28,28},{1,1},{5... | collective-permute-start | bytes 1572872 | tf_op jit(solution)/shard_map/ppermute | solution.py:1581
